TPU v7x, 32 devices: a whole 2x2x4 slice. The times are simulated.
32 devices in a mesh: dp: 8 (over y, x, core), mp: 4 (over z).
Axes of the slice: x: 2, y: 2, z: 4, core: 2. Of those that a mesh axis runs over, the one named last changes fastest.
Arguments:
- cells: bfloat16 [16, 1024, 1024], P('dp', 'mp'), may hold values from -6 to 6
- lengths: int32 [16], P('dp'), may hold values from 256 to 1024, as said below
- query_matrix: bfloat16 [1024, 1024], P(None, 'mp'), may hold values from -0.1875 to 0.1875
- key_matrix: bfloat16 [1024, 1024], P(None, 'mp'), may hold values from -0.1875 to 0.1875
- value_matrix: bfloat16 [1024, 1024], P(None, 'mp'), may hold values from -0.1875 to 0.1875
- query_bias: float32 [1024], P('mp'), may hold values from -3 to 3
- value_bias: float32 [1024], P('mp'), may hold values from -3 to 3
- output_matrix: bfloat16 [1024, 1024], P('mp'), may hold values from -1.5 to 1.5
- b_out: float32 [1024], replicated, may hold values from -2 to 2
- gain_one: float32 [1024], replicated, may hold values from 0.5 to 1.5
- shift_one: float32 [1024], replicated, may hold values from -2 to 2
- gain_two: float32 [1024], replicated, may hold values from 0.5 to 1.5
- shift_two: float32 [1024], replicated, may hold values from -2 to 2
- expand_weight: bfloat16 [1024, 4096], P(None, 'mp'), may hold values from -0.1875 to 0.1875
- expand_bias: float32 [4096], P('mp'), may hold values from -3 to 3
- contract_weight: bfloat16 [4096, 1024], P('mp'), may hold values from -0.09375 to 0.09375
- b_down: float32 [1024], replicated, may hold values from -2 to 2
- grad_out: bfloat16 [16, 1024, 1024], P('dp', 'mp'), may hold values from -6 to 6
Outputs:
- out_cells: bfloat16 [16, 1024, 1024], P('dp', 'mp')
- grad_cells: float32 [16, 1024, 1024], P('dp', 'mp')
- grad_w_query: float32 [1024, 1024], P('dp', 'mp')
- grad_w_key: float32 [1024, 1024], P('dp', 'mp')
- grad_w_value: float32 [1024, 1024], P('dp', 'mp')
- grad_b_query: float32 [1024], P(('mp', 'dp'))
- grad_b_value: float32 [1024], P(('mp', 'dp'))
- grad_w_out: float32 [1024, 1024], P('mp', 'dp')
- grad_b_out: float32 [1024], P(('dp', 'mp'))
- grad_gain_one: float32 [1024], P(('dp', 'mp'))
- grad_shift_one: float32 [1024], P(('dp', 'mp'))
- grad_gain_two: float32 [1024], P(('dp', 'mp'))
- grad_shift_two: float32 [1024], P(('dp', 'mp'))
- grad_w_up: float32 [1024, 4096], P('dp', 'mp')
- grad_b_up: float32 [4096], P(('mp', 'dp'))
- grad_w_down: float32 [4096, 1024], P('mp', 'dp')
- grad_b_down: float32 [1024], P(('dp', 'mp'))
Inputs may be any that keep to these rules, and one draw needn't show every extreme that they name: `lengths`: among the 2 slides of each index of dp, one, drawn from the seed, has exactly 1024 cells.
All inputs are finite; a program needn't handle non-finite values.
Results may differ from a plain program's by a relative error of at most 0.019.
Values may be sent and summed in bfloat16 or wider, within the bound.
A program may use at most 192 MiB of HBM per device.

v0:
```python
from functools import partial

import jax
import jax.numpy as jnp
from jax import lax
from jax.sharding import PartitionSpec as P

HD = 64


epsilon = 1e-05


def layer_norm(values, norm_gain, norm_shift):
    center = values - jnp.mean(values, -1, keepdims=True)
    inverse = lax.rsqrt(jnp.mean(center * center, -1, keepdims=True) + epsilon)
    normed = center * inverse
    return (normed * norm_gain + norm_shift, normed, inverse)


def norm_back(upstream, normed, inverse, norm_gain):
    scaled = upstream * norm_gain
    return inverse * (
        scaled
        - jnp.mean(scaled, -1, keepdims=True)
        - normed * jnp.mean(scaled * normed, -1, keepdims=True)
    )


def gelu_pair(values):
    cumulative = 0.5 * (1.0 + lax.erf(values * 0.7071067811865476))
    density = jnp.exp(-0.5 * values * values) * 0.3989422804014327
    return (values * cumulative, cumulative + values * density)


def scores_of(query_rows, key_inputs, allowed, factor):
    scores = (
        jnp.einsum("qhd,khd->hqk", query_rows, key_inputs, preferred_element_type=jnp.float32)
        * factor
    )
    return jnp.where(allowed[None, None, :], scores, -1e30)


def attend_forward(factor, packed):
    query_rows, key_inputs, value_inputs, allowed = packed
    scores = scores_of(query_rows, key_inputs, allowed, factor)
    row_top = jnp.max(scores, -1, keepdims=True)
    lifted = jnp.exp(scores - row_top)
    row_total = jnp.sum(lifted, -1, keepdims=True)
    soft_rows = lifted / row_total
    blended_heads = jnp.einsum(
        "hqk,khd->qhd",
        soft_rows.astype(jnp.bfloat16),
        value_inputs,
        preferred_element_type=jnp.float32,
    )
    return (blended_heads.astype(jnp.bfloat16), row_top + jnp.log(row_total))


def attend_backward(factor, packed):
    query_rows, key_inputs, value_inputs, allowed, logsum, d_mixed = packed
    soft_rows = jnp.exp(scores_of(query_rows, key_inputs, allowed, factor) - logsum)
    d_soft = jnp.einsum("qhd,khd->hqk", d_mixed, value_inputs, preferred_element_type=jnp.float32)
    value_gradient = jnp.einsum(
        "hqk,qhd->khd", soft_rows.astype(jnp.bfloat16), d_mixed, preferred_element_type=jnp.float32
    )
    d_scores = (soft_rows * (d_soft - jnp.sum(d_soft * soft_rows, -1, keepdims=True))).astype(
        jnp.bfloat16
    )
    query_gradient = (
        jnp.einsum("hqk,khd->qhd", d_scores, key_inputs, preferred_element_type=jnp.float32)
        * factor
    )
    key_gradient = (
        jnp.einsum("hqk,qhd->khd", d_scores, query_rows, preferred_element_type=jnp.float32)
        * factor
    )
    return (
        query_gradient.astype(jnp.bfloat16),
        key_gradient.astype(jnp.bfloat16),
        value_gradient.astype(jnp.bfloat16),
    )


def body(
    cells,
    lengths,
    query_matrix,
    key_matrix,
    value_matrix,
    query_bias,
    value_bias,
    output_matrix,
    b_out,
    gain_one,
    shift_one,
    gain_two,
    shift_two,
    expand_weight,
    expand_bias,
    contract_weight,
    b_down,
    grad_out,
):
    number_slides, local_rows, model_width = cells.shape
    full_rows = local_rows * lax.axis_size("mp")
    head_count = query_matrix.shape[1] // HD
    factor = HD ** (-0.5)
    first_row = lax.axis_index("mp") * local_rows
    allowed = jnp.arange(full_rows)[None, :] < lengths[:, None]
    cells_all, grad_all = (
        lax.all_gather(cells, "mp", axis=1, tiled=True),
        lax.all_gather(grad_out, "mp", axis=1, tiled=True),
    )
    keep_rows = allowed.astype(jnp.float32)[:, :, None]
    residual = cells_all.astype(jnp.float32)
    out_grad = keep_rows * grad_all.astype(jnp.float32)
    normed_in, unit_one, inverse_one = layer_norm(residual, gain_one, shift_one)
    first_rows = normed_in.astype(jnp.bfloat16)
    adjoint_rows = out_grad.astype(jnp.bfloat16)
    head_shape = (number_slides, full_rows, head_count, HD)
    query_rows = (
        (
            jnp.einsum("ujg,gm->ujm", first_rows, query_matrix, preferred_element_type=jnp.float32)
            + query_bias
        )
        .astype(jnp.bfloat16)
        .reshape(head_shape)
    )
    key_inputs = (
        jnp.einsum("ujg,gm->ujm", first_rows, key_matrix, preferred_element_type=jnp.float32)
        .astype(jnp.bfloat16)
        .reshape(head_shape)
    )
    value_inputs = (
        (
            jnp.einsum("ujg,gm->ujm", first_rows, value_matrix, preferred_element_type=jnp.float32)
            + value_bias
        )
        .astype(jnp.bfloat16)
        .reshape(head_shape)
    )
    blended_heads, logsum = lax.map(
        partial(attend_forward, factor), (query_rows, key_inputs, value_inputs, allowed)
    )
    blended_flat = blended_heads.reshape(number_slides, full_rows, head_count * HD)
    attention_piece = jnp.einsum(
        "tbk,kf->tbf", blended_flat, output_matrix, preferred_element_type=jnp.float32
    )
    attention_total = lax.psum(attention_piece, "mp")
    middle = residual + attention_total + b_out
    normed_mid, unit_two, inverse_two = layer_norm(middle, gain_two, shift_two)
    second_rows = normed_mid.astype(jnp.bfloat16)
    expanded_rows = (
        jnp.einsum("uwz,zo->uwo", second_rows, expand_weight, preferred_element_type=jnp.float32)
        + expand_bias
    )
    hidden_activated, slope = gelu_pair(expanded_rows)
    hidden_reduced = hidden_activated.astype(jnp.bfloat16)
    contract_piece = jnp.einsum(
        "ptm,mz->ptz", hidden_reduced, contract_weight, preferred_element_type=jnp.float32
    )
    contract_total = lax.psum(contract_piece.astype(jnp.bfloat16), "mp").astype(jnp.float32)
    result = keep_rows * (middle + contract_total + b_down)
    grad_w_down_local = jnp.einsum(
        "czy,czh->yh", hidden_reduced, adjoint_rows, preferred_element_type=jnp.float32
    )
    hidden_gradient = jnp.einsum(
        "jnm,rm->jnr", adjoint_rows, contract_weight, preferred_element_type=jnp.float32
    )
    upper_gradient = (hidden_gradient * slope).astype(jnp.bfloat16)
    grad_w_up_local = jnp.einsum(
        "iem,iev->mv", second_rows, upper_gradient, preferred_element_type=jnp.float32
    )
    grad_b_up_local = jnp.sum(upper_gradient.astype(jnp.float32), (0, 1))
    second_row_gradient = jnp.einsum(
        "trn,en->tre", upper_gradient, expand_weight, preferred_element_type=jnp.float32
    )
    d_norm_two = lax.psum(second_row_gradient, "mp")
    d_middle = out_grad + norm_back(d_norm_two, unit_two, inverse_two, gain_two)
    between_rows = d_middle.astype(jnp.bfloat16)
    grad_w_out_local = jnp.einsum(
        "zgn,zgi->ni", blended_flat, between_rows, preferred_element_type=jnp.float32
    )
    d_mixed = (
        jnp.einsum("xqb,mb->xqm", between_rows, output_matrix, preferred_element_type=jnp.float32)
        .astype(jnp.bfloat16)
        .reshape(head_shape)
    )
    query_gradient, key_gradient, value_gradient = lax.map(
        partial(attend_backward, factor),
        (query_rows, key_inputs, value_inputs, allowed, logsum, d_mixed),
    )
    flat_shape = (number_slides, full_rows, head_count * HD)
    query_gradient = query_gradient.reshape(flat_shape)
    key_gradient = key_gradient.reshape(flat_shape)
    value_gradient = value_gradient.reshape(flat_shape)
    grad_w_query_local = jnp.einsum(
        "qxa,qxb->ab", first_rows, query_gradient, preferred_element_type=jnp.float32
    )
    grad_w_key_local = jnp.einsum(
        "qxa,qxb->ab", first_rows, key_gradient, preferred_element_type=jnp.float32
    )
    grad_w_value_local = jnp.einsum(
        "qxa,qxb->ab", first_rows, value_gradient, preferred_element_type=jnp.float32
    )
    grad_b_query_local = jnp.sum(query_gradient.astype(jnp.float32), (0, 1))
    grad_b_value_local = jnp.sum(value_gradient.astype(jnp.float32), (0, 1))
    d_rows_one = (
        jnp.einsum("rzo,ho->rzh", query_gradient, query_matrix, preferred_element_type=jnp.float32)
        + jnp.einsum("rzo,ho->rzh", key_gradient, key_matrix, preferred_element_type=jnp.float32)
        + jnp.einsum(
            "rzo,ho->rzh", value_gradient, value_matrix, preferred_element_type=jnp.float32
        )
    )
    d_norm_one = lax.psum(d_rows_one, "mp")
    pick = partial(lax.dynamic_slice_in_dim, start_index=first_row, slice_size=local_rows, axis=1)
    d_cells = d_middle + norm_back(d_norm_one, unit_one, inverse_one, gain_one)
    weight_sums = (
        lax.psum_scatter(grad_w_query_local, "dp", scatter_dimension=0, tiled=True),
        lax.psum_scatter(grad_w_key_local, "dp", scatter_dimension=0, tiled=True),
        lax.psum_scatter(grad_w_value_local, "dp", scatter_dimension=0, tiled=True),
        lax.psum_scatter(grad_b_query_local, "dp", scatter_dimension=0, tiled=True),
        lax.psum_scatter(grad_b_value_local, "dp", scatter_dimension=0, tiled=True),
        lax.psum_scatter(grad_w_out_local, "dp", scatter_dimension=1, tiled=True),
        lax.psum_scatter(grad_w_up_local, "dp", scatter_dimension=0, tiled=True),
        lax.psum_scatter(grad_b_up_local, "dp", scatter_dimension=0, tiled=True),
        lax.psum_scatter(grad_w_down_local, "dp", scatter_dimension=1, tiled=True),
    )
    vector_sums = (
        lax.psum_scatter(
            jnp.sum(pick(d_middle), (0, 1)), ("dp", "mp"), scatter_dimension=0, tiled=True
        ),
        lax.psum_scatter(
            jnp.sum(pick(d_norm_one * unit_one), (0, 1)),
            ("dp", "mp"),
            scatter_dimension=0,
            tiled=True,
        ),
        lax.psum_scatter(
            jnp.sum(pick(d_norm_one), (0, 1)), ("dp", "mp"), scatter_dimension=0, tiled=True
        ),
        lax.psum_scatter(
            jnp.sum(pick(d_norm_two * unit_two), (0, 1)),
            ("dp", "mp"),
            scatter_dimension=0,
            tiled=True,
        ),
        lax.psum_scatter(
            jnp.sum(pick(d_norm_two), (0, 1)), ("dp", "mp"), scatter_dimension=0, tiled=True
        ),
        lax.psum_scatter(
            jnp.sum(pick(out_grad), (0, 1)), ("dp", "mp"), scatter_dimension=0, tiled=True
        ),
    )
    return (
        pick(result).astype(jnp.bfloat16),
        pick(d_cells),
        weight_sums[0],
        weight_sums[1],
        weight_sums[2],
        weight_sums[3],
        weight_sums[4],
        weight_sums[5],
        vector_sums[0],
        vector_sums[1],
        vector_sums[2],
        vector_sums[3],
        vector_sums[4],
        weight_sums[6],
        weight_sums[7],
        weight_sums[8],
        vector_sums[5],
    )


def solution(mesh):
    placed = (
        P("dp", "mp", None),
        P("dp"),
        P(None, "mp"),
        P(None, "mp"),
        P(None, "mp"),
        P("mp"),
        P("mp"),
        P("mp", None),
        P(),
        P(),
        P(),
        P(),
        P(),
        P(None, "mp"),
        P("mp"),
        P("mp", None),
        P(),
        P("dp", "mp", None),
    )
    return jax.shard_map(
        body,
        mesh=mesh,
        in_specs=placed,
        out_specs=(
            P("dp", "mp", None),
            P("dp", "mp", None),
            P("dp", "mp"),
            P("dp", "mp"),
            P("dp", "mp"),
            P(("mp", "dp")),
            P(("mp", "dp")),
            P("mp", "dp"),
            P(("dp", "mp")),
            P(("dp", "mp")),
            P(("dp", "mp")),
            P(("dp", "mp")),
            P(("dp", "mp")),
            P("dp", "mp"),
            P(("mp", "dp")),
            P("mp", "dp"),
            P(("dp", "mp")),
        ),
        check_vma=False,
    )
```

profile of v0, /device:TPU:9, one launch (start us, length us, event | category | flops | bytes accessed | tf_op | source)
XLA Modules:
  0.0 1547.8 jit_solution(5787183834978732004)
XLA Ops:
  9.3 79.7 %all-gather.3.cloned.1.call-done = bf16[2,1024,1024]{2,1,0:T(8,128)(2,1)} async-done(((bf16[2,256,1024]{2,1,0:T(8,128)(2,1)}), bf16[2,1024,1024]{2,1,0:T(8,128)(2,1)}) %all-gather.3.cloned.1.call-update) | async-done | bytes 4194320 | tf_op jit(solution)/shard_map/all_gather | solution.py:112
  89.1 3.0 convert_reduce_fusion
  92.1 3.0 fusion.56
  95.1 2.6 convolution_convert_fusion.1
  97.8 3.3 add_convert_fusion.3
  101.1 3.4 add_convert_fusion.2
  105.6 27.1 %while.26 = (s32[]{:T(128)}, bf16[2,1024,4,64]{1,3,2,0:T(8,128)(2,1)}, f32[2,4,1024,1]{2,1,3,0:T(4,128)S(1)}, bf16[2,1024,4,64]{1,3,2,0:T(8,128)(2,1)}, pred[2,1...) while((s32[]{:T(128)}, ...), condition=%wide.region_5.6_spmd, body=%wide.region_2.5_spmd.sunk | while | flops 1124331520 | bytes 65150136 | solution.py:143
  105.9 4.2 fusion.139
  110.1 4.0 fusion.140
  114.1 4.2 fusion.141
  119.3 4.2 fusion.139
  123.5 4.0 fusion.140
  127.5 4.2 fusion.141
  132.7 5.9 fusion.95
  139.3 289.2 %all-reduce.16.cloned.1.call-done = f32[2,1024,1024]{2,1,0:T(8,128)} async-done(((f32[2,1024,1024]{2,1,0:T(8,128)}), f32[2,1024,1024]{2,1,0:T(8,128)}) %all-reduce.16.cloned.1.call-update) | async-done | bytes 8388624 | tf_op jit(solution)/shard_map/psum | solution.py:150
  428.6 5.8 fusion.107
  434.3 1.6 multiply_reduce_fusion.3
  437.5 3.6 copy-done.9
  441.1 7.8 multiply_convert_fusion.1
  448.9 60.6 %all-gather.5.cloned.1.call-done = bf16[2,1024,1024]{2,1,0:T(8,128)(2,1)} async-done(((bf16[2,256,1024]{2,1,0:T(8,128)(2,1)}), bf16[2,1024,1024]{2,1,0:T(8,128)(2,1)}) %all-gather.5.cloned.1.call-update) | async-done | bytes 4194320 | tf_op jit(solution)/shard_map/all_gather | solution.py:113
  509.5 11.5 convert_reduce_fusion.1
  520.9 2.0 copy-done.48
  522.9 6.8 fusion.80
  531.3 8.3 convolution_convert_fusion
  539.7 280.1 %all-reduce.20.cloned.1.call-done = f32[2,1024,1024]{2,1,0:T(8,128)} async-done(((f32[2,1024,1024]{2,1,0:T(8,128)}), f32[2,1024,1024]{2,1,0:T(8,128)}) %all-reduce.20.cloned.1.call-update) | async-done | bytes 8388624 | tf_op jit(solution)/shard_map/psum | solution.py:179
  819.8 7.3 multiply_reduce_fusion.4
  829.3 9.8 convert_multiply_fusion
  839.1 3.2 copy-done.3
  847.0 63.8 %while.27 = (s32[]{:T(128)}, bf16[2,1024,4,64]{1,3,2,0:T(8,128)(2,1)}, bf16[2,1024,4,64]{1,3,2,0:T(8,128)(2,1)}, bf16[2,1024,4,64]{1,3,2,0:T(8,128)(2,1)}, bf16[...) while((s32[]{:T(128)}, ...), condition=%wide.region_15.16_spmd, body=%wide.region_13.15_spmd.sunk | while | flops 2723409920 | bytes 147939568 | solution.py:190
  848.1 5.1 subtract_exponential_fusion.3
  853.2 3.5 fusion.152
  856.7 8.2 multiply_reduce_fusion.7
  864.9 7.9 multiply_convert_fusion.3
  872.8 3.5 fusion.151
  876.3 1.6 fusion.150
  879.9 5.1 subtract_exponential_fusion.3
  885.0 3.5 fusion.152
  888.5 8.2 multiply_reduce_fusion.7
  896.7 7.8 multiply_convert_fusion.3
  904.5 3.5 fusion.151
  908.0 1.6 fusion.150
  910.9 2.8 fusion.100
  915.0 4.6 add_add_fusion
  920.4 11.1 convolution_bitcast_fusion
  932.0 10.2 fusion.68
  942.3 5.7 fusion.91
  948.1 5.4 convolution_bitcast_fusion.1
  953.6 5.4 convolution_bitcast_fusion.2
  961.0 15.0 all-reduce.18.cloned.1.call-done
  976.1 3.1 fusion.77
  979.7 12.1 all-reduce.10
  993.6 1.7 dynamic-slice_reduce_fusion.2
  995.4 5.4 convolution_bitcast_fusion.3
  1000.8 2.6 dynamic-slice_reduce_fusion.3
  1003.4 265.0 %all-reduce.22.cloned.1.call-done = f32[2,1024,1024]{2,1,0:T(8,128)} async-done(((f32[2,1024,1024]{2,1,0:T(8,128)}), f32[2,1024,1024]{2,1,0:T(8,128)}) %all-reduce.22.cloned.1.call-update) | async-done | bytes 8388624 | tf_op jit(solution)/shard_map/psum | solution.py:216
  1268.4 6.3 fusion.106
  1274.7 4.3 dynamic-slice_reduce_fusion.4
  1279.0 41.3 %all-reduce.9 = (f32[1024]{0:T(1024)S(1)}, f32[1024]{0:T(1024)S(1)}, f32[1024]{0:T(1024)S(1)}, f32[1024]{0:T(1024)S(1)}, f32[1024]{0:T(1024)S(1)}, /*index=5*/f32[1024]{0:T(1024)S(1)}) all-reduce(f32[1024]{0:T(1024)S(1)} %get-tuple-element.173, f32[1024]{0:T(1024)S(1)} %get-tuple-element.119, ...), channel_id=8, replica_groups=mesh['dp'=8,'mp'=4] {'dp','mp'}, use_global_device_ids=true, to_apply=%region_28.29.clone | all-reduce | flops 6144 | bytes 49152
  1323.8 1.8 reduce-scatter.15.cloned.1.call-done
  1325.5 55.1 %reduce-scatter.17.cloned.1.call-done = f32[1024,128]{1,0:T(8,128)} async-done(((f32[1024,1024]{1,0:T(8,128)}), f32[1024,128]{1,0:T(8,128)}) %reduce-scatter.17.cloned.1.call-update) | async-done | bytes 524304 | tf_op jit(solution)/shard_map/reduce_scatter | solution.py:228
  1380.6 40.0 %reduce-scatter.13.cloned.1.call-done = f32[256,128]{1,0:T(8,128)} async-done(((f32[256,1024]{1,0:T(8,128)}), f32[256,128]{1,0:T(8,128)}) %reduce-scatter.13.cloned.1.call-update) | async-done | bytes 131088 | tf_op jit(solution)/shard_map/reduce_scatter | solution.py:225
  1420.6 40.0 %reduce-scatter.11.cloned.1.call-done = f32[128,256]{1,0:T(8,128)} async-done(((f32[1024,256]{1,0:T(8,128)}), f32[128,256]{1,0:T(8,128)}) %reduce-scatter.11.cloned.1.call-update) | async-done | bytes 131088 | tf_op jit(solution)/shard_map/reduce_scatter | solution.py:222
  1460.6 40.1 %reduce-scatter.9.cloned.1.call-done = f32[128,256]{1,0:T(8,128)} async-done(((f32[1024,256]{1,0:T(8,128)}), f32[128,256]{1,0:T(8,128)}) %reduce-scatter.9.cloned.1.call-update) | async-done | bytes 131088 | tf_op jit(solution)/shard_map/reduce_scatter | solution.py:221
  1500.8 40.0 %reduce-scatter.7.cloned.1.call-done = f32[128,256]{1,0:T(8,128)} async-done(((f32[1024,256]{1,0:T(8,128)}), f32[128,256]{1,0:T(8,128)}) %reduce-scatter.7.cloned.1.call-update) | async-done | bytes 131088 | tf_op jit(solution)/shard_map/reduce_scatter | solution.py:220
  (174 shorter events, 29.2 us)
Async XLA Ops:
  7.2 433.9 %copy-start = (bf16[1024,1024]{1,0:T(8,128)(2,1)S(1)}, bf16[1024,1024]{1,0:T(8,128)(2,1)}, u32[]{:S(2)}) copy-start(bf16[1024,1024]{1,0:T(8,128)(2,1)} %param.35) | copy-start | bytes 6291460
  7.2 87.9 %copy-start.35 = (f32[1024]{0:T(1024)S(1)}, f32[1024]{0:T(1024)}, u32[]{:S(2)}) copy-start(f32[1024]{0:T(1024)} %param.31) | copy-start | bytes 12292
  7.2 87.9 %copy-start.43 = (f32[1024]{0:T(1024)S(1)}, f32[1024]{0:T(1024)}, u32[]{:S(2)}) copy-start(f32[1024]{0:T(1024)} %param.32) | copy-start | bytes 12292
  7.2 81.8 %all-gather.3.cloned.1.call-start = ((), (), s32[]{:S(2)}) async-start(), calls=%async_computation.6 | async-start | bytes 5242880 | tf_op jit(solution)/shard_map/all_gather | solution.py:112
  8.0 420.6 %all-reduce.16.cloned.1.call-start = ((), (), s32[]{:S(2)}) async-start(), calls=%async_computation.7 | async-start | bytes 16777216 | tf_op jit(solution)/shard_map/psum | solution.py:150
  89.1 6.1 copy-start.4
  89.1 6.1 copy-start.22
  92.0 9.0 copy-start.26
  95.1 2.7 copy-start.24
  95.1 2.7 copy-start.45
  95.1 6.0 copy-start.28
  97.7 3.4 copy-start.21
  97.7 3.4 copy-start.46
  110.1 4.0 copy-start.10
  110.1 4.0 copy-start.17
  118.3 1.0 copy-start.11
  123.5 4.0 copy-start.10
  123.5 4.0 copy-start.17
  131.7 1.0 copy-start.11
  132.7 295.9 %copy-start.38 = (f32[1024]{0:T(1024)S(1)}, f32[1024]{0:T(1024)}, u32[]{:S(2)}) copy-start(f32[1024]{0:T(1024)} %param.30) | copy-start | bytes 12292
  138.6 370.9 %all-gather.5.cloned.1.call-start = ((), (), s32[]{:S(2)}) async-start(), calls=%async_computation.9 | async-start | bytes 5242880 | tf_op jit(solution)/shard_map/all_gather | solution.py:113
  139.3 680.5 %all-reduce.20.cloned.1.call-start = ((), (), s32[]{:S(2)}) async-start(), calls=%async_computation.10 | async-start | bytes 16777216 | tf_op jit(solution)/shard_map/psum | solution.py:179
  434.3 3.2 copy-start.2
  436.0 5.1 copy-start.32
  436.0 5.1 copy-start.40
  436.0 5.1 copy-start.41
  437.5 3.6 copy-start.9
  441.1 68.4 %copy-start.30 = (f32[2,1024]{1,0:T(2,128)S(1)}, f32[2,1024]{1,0:T(2,128)}, u32[]{:S(2)}) copy-start(f32[2,1024]{1,0:T(2,128)} %get-tuple-element.177) | copy-start | bytes 24580
  520.9 2.0 copy-start.48
  529.8 1.6 copy-start.39
  529.8 446.3 %all-reduce.18.cloned.1.call-start = ((), (), s32[]{:S(2)}) async-start(), calls=%async_computation.8 | async-start | bytes 8388608 | tf_op jit(solution)/shard_map/psum | solution.py:163
  539.7 728.7 %all-reduce.22.cloned.1.call-start = ((), (), s32[]{:S(2)}) async-start(), calls=%async_computation.11 | async-start | bytes 16777216 | tf_op jit(solution)/shard_map/psum | solution.py:216
  819.8 8.2 copy-start.5
  819.8 9.5 copy-start.18
  829.3 13.1 copy-start.20
  839.1 3.2 copy-start.3
  839.1 7.9 copy-start.8
  872.8 3.5 copy-start.7
  872.8 3.5 copy-start.14
  877.9 1.0 copy-start.15
  904.5 3.5 copy-start.7
  904.5 3.5 copy-start.14
  909.6 1.0 copy-start.15
  910.8 2.9 copy-start.19
  910.8 2.9 copy-start.23
  910.8 4.2 copy-start.13
  910.8 4.2 copy-start.25
  919.7 12.3 copy-start.31
  919.7 405.8 %reduce-scatter.15.cloned.1.call-start = ((), (), s32[]{:S(2)}) async-start(), calls=%async_computation.16 | async-start | bytes 4718592 | tf_op jit(solution)/shard_map/reduce_scatter | solution.py:226
  931.5 10.7 copy-start.12
  931.6 449.1 %reduce-scatter.17.cloned.1.call-start = ((), (), s32[]{:S(2)}) async-start(), calls=%async_computation.17 | async-start | bytes 4718592 | tf_op jit(solution)/shard_map/reduce_scatter | solution.py:228
  942.2 5.9 copy-start.27
  942.2 5.9 copy-start.29
  942.2 5.9 copy-start.36
  942.2 5.9 copy-start.44
  942.2 478.4 %reduce-scatter.13.cloned.1.call-start = ((), (), s32[]{:S(2)}) async-start(), calls=%async_computation.15 | async-start | bytes 1179648 | tf_op jit(solution)/shard_map/reduce_scatter | solution.py:225
  948.0 512.6 %reduce-scatter.11.cloned.1.call-start = ((), (), s32[]{:S(2)}) async-start(), calls=%async_computation.14 | async-start | bytes 1179648 | tf_op jit(solution)/shard_map/reduce_scatter | solution.py:222
  953.5 5.6 copy-start.47
  953.5 22.6 %copy-start.34 = (f32[1024]{0:T(1024)S(1)}, f32[1024]{0:T(1024)}, u32[]{:S(2)}) copy-start(f32[1024]{0:T(1024)} %param.38) | copy-start | bytes 12292
  953.5 25.7 %copy-start.16 = (bf16[2,1024,4,64]{1,3,2,0:T(8,128)(2,1)S(1)}, bf16[2,1024,4,64]{1,3,2,0:T(8,128)(2,1)}, u32[]{:S(2)}) copy-start(bf16[2,1024,4,64]{1,3,2,0:T(8,128)(2,1)} %get-tuple-element.111) | copy-start | bytes 3145732
  953.5 26.2 %copy-start.37 = (f32[1024]{0:T(1024)S(1)}, f32[1024]{0:T(1024)}, u32[]{:S(2)}) copy-start(f32[1024]{0:T(1024)} %get-tuple-element.181) | copy-start | bytes 12292
  953.5 547.2 %reduce-scatter.9.cloned.1.call-start = ((), (), s32[]{:S(2)}) async-start(), calls=%async_computation.13 | async-start | bytes 1179648 | tf_op jit(solution)/shard_map/reduce_scatter | solution.py:221
  959.0 581.7 %reduce-scatter.7.cloned.1.call-start = ((), (), s32[]{:S(2)}) async-start(), calls=%async_computation.12 | async-start | bytes 1179648 | tf_op jit(solution)/shard_map/reduce_scatter | solution.py:220
  1268.4 272.4 %copy-start.1 = (bf16[1024,1024]{1,0:T(8,128)(2,1)S(1)}, bf16[1024,1024]{1,0:T(8,128)(2,1)}, u32[]{:S(2)}) copy-start(bf16[1024,1024]{1,0:T(8,128)(2,1)} %param.35) | copy-start | bytes 6291460
  (4 other events, 3.3 us)
Sparse Core Ops, SparseCore 0:
  9.6 79.3 all-gather.2
  138.7 289.8 all-reduce.15
  430.1 79.2 all-gather.4
  529.9 289.8 all-reduce.19
  822.0 154.0 all-reduce.17
  978.5 289.7 all-reduce.21
  1272.7 52.8 reduce-scatter.14
  1329.5 51.1 reduce-scatter.16
  1384.7 35.9 reduce-scatter.12
  1424.6 36.0 reduce-scatter.10
  1464.7 36.0 reduce-scatter.8
  1504.7 36.0 reduce-scatter.6
where the time goes:
time: 1550 us
  waiting for transfers between devices  1210 us (78%)
  matrix products  163 us (11%)
  other arithmetic  74.9 us (5%)
  blocking collectives  53.4 us (3%)
  local copies, waits for them, and re-layouts  30.2 us (2%)
  between operations  16.3 us (1%)
    psum x1, waiting for transfers between devices, body(): attention_total = lax.psum(attention_piece, 'mp')  289 us
    psum x1, waiting for transfers between devices, body(): d_norm_two = lax.psum(second_row_gradient, 'mp')  280 us
    psum x1, waiting for transfers between devices, body(): d_norm_one = lax.psum(d_rows_one, 'mp')  265 us
    all_gather x1, waiting for transfers between devices, body(): lax.all_gather(cells, 'mp', axis=1, tiled=True)  79.7 us
    all_gather x1, waiting for transfers between devices, body(): lax.all_gather(grad_out, 'mp', axis=1, tiled=True)  60.6 us
    reduce_scatter x1, waiting for transfers between devices, body(): lax.psum_scatter(grad_w_down_local, 'dp', scatter_dimension=1, tiled=True)  55.1 us
    unnamed x2, blocking collectives  53.4 us
    reduce_scatter x1, waiting for transfers between devices, body(): lax.psum_scatter(grad_w_key_local, 'dp', scatter_dimension=0, tiled=True)  40.1 us
  transfers between devices with their start and end apart: 12, of which 12 were waited for; matrix products, arithmetic and copies ran while one was open for 12% of the time, Pallas kernels for 0%

commit v1 on v0

v1 whole, which is shorter than its diff:
```python
import jax
import jax.numpy as jnp
from jax import lax
from jax.sharding import PartitionSpec as P

HD = 64
EPS = 1e-05
BF = jnp.bfloat16
F32 = jnp.float32


def dot(a, b, ca, cb):
    return lax.dot_general(a, b, (((ca,), (cb,)), ((), ())), preferred_element_type=F32)


def cross(x, bit):
    n = lax.axis_size("dp")
    return lax.ppermute(x, "dp", [(i, i ^ (1 << bit)) for i in range(n)])


def shift(x, by):
    n = lax.axis_size("mp")
    return lax.ppermute(x, "mp", [(i, (i + by) % n) for i in range(n)])


def moves(n_dp, n_mp, slots):
    per = n_mp // slots
    turns = []
    for t in range(slots):
        pairs = []
        for d in range(n_dp):
            for m in range(n_mp):
                s = (t + m) % slots
                base, c = d - d % per, d % per
                target = (base + m // slots, c * slots + s)
                pairs.append((d * n_mp + m, target[0] * n_mp + target[1]))
        turns.append(pairs)
    return turns


def plane_bits(n_dp, flip):
    bits = list(range(1, n_dp.bit_length() - 1))
    return bits[::-1] if flip else bits


def gather(piece, flip):
    n_dp, n_mp = lax.axis_size("dp"), lax.axis_size("mp")
    stack = jnp.stack([shift(piece, n_mp - r) for r in range(1, n_mp)])
    held = {0: stack}
    for bit in plane_bits(n_dp, flip) + [0]:
        held.update({i ^ (1 << bit): cross(v, bit) for i, v in list(held.items())})
    return held


def assemble(held, own, d):
    n = len(held)
    stack = jnp.stack([held[i] for i in range(n)])
    order = jnp.arange(n) ^ d
    placed = jnp.take(stack, order, axis=0)
    placed = jnp.moveaxis(placed, 0, 1).reshape((stack.shape[1], -1, stack.shape[-1]))
    return [own] + [placed[r] for r in range(placed.shape[0])]


def scatter(blocks, flip):
    n_dp = lax.axis_size("dp")
    for bit in plane_bits(n_dp, flip):
        keep = sorted(i for i in blocks if not i >> bit & 1)
        got = cross(jnp.stack([blocks[i ^ (1 << bit)] for i in keep]), bit)
        blocks = {
            i: (blocks[i].astype(F32) + got[k].astype(F32)).astype(blocks[i].dtype)
            for k, i in enumerate(keep)
        }
    return blocks[0]


def layer_norm(v, gain, bias):
    center = v - jnp.mean(v, -1, keepdims=True)
    inverse = lax.rsqrt(jnp.mean(center * center, -1, keepdims=True) + EPS)
    unit = center * inverse
    return unit * gain + bias, unit, inverse


def norm_back(up, unit, inverse, gain):
    u = up * gain
    return inverse * (
        u - jnp.mean(u, -1, keepdims=True) - unit * jnp.mean(u * unit, -1, keepdims=True)
    )


def gelu_pair(v):
    cumulative = 0.5 * (1.0 + lax.erf(v * 0.7071067811865476))
    density = jnp.exp(-0.5 * v * v) * 0.3989422804014327
    return v * cumulative, cumulative + v * density


def attend(q, k, v, allowed):
    heads = q.shape[1] // HD
    qh = q.reshape(-1, heads, HD)
    kh = k.reshape(-1, heads, HD)
    vh = v.reshape(-1, heads, HD)
    s = jnp.einsum("qhd,khd->hqk", qh, kh, preferred_element_type=F32) * HD**-0.5
    s = jnp.where(allowed[None, None, :], s, -1e30)
    e = jnp.exp(s - jnp.max(s, -1, keepdims=True))
    p = (e / jnp.sum(e, -1, keepdims=True)).astype(BF)
    mixed = jnp.einsum("hqk,khd->qhd", p, vh, preferred_element_type=F32)
    return mixed.astype(BF).reshape(q.shape), p


def attend_back(q, k, v, p, mixed, dm):
    heads = q.shape[1] // HD
    qh = q.reshape(-1, heads, HD)
    kh = k.reshape(-1, heads, HD)
    vh = v.reshape(-1, heads, HD)
    dh = dm.reshape(-1, heads, HD)
    pf = p.astype(F32)
    dp = jnp.einsum("qhd,khd->hqk", dh, vh, preferred_element_type=F32)
    total = jnp.sum(dp * pf, -1, keepdims=True)
    ds = (pf * (dp - total)).astype(BF)
    dv = jnp.einsum("hqk,qhd->khd", p, dh, preferred_element_type=F32)
    dq = jnp.einsum("hqk,khd->qhd", ds, kh, preferred_element_type=F32) * HD**-0.5
    dk = jnp.einsum("hqk,qhd->khd", ds, qh, preferred_element_type=F32) * HD**-0.5
    return (
        dq.astype(BF).reshape(q.shape),
        dk.astype(BF).reshape(k.shape),
        dv.astype(BF).reshape(k.shape),
    )


def body(
    cells,
    lengths,
    query_matrix,
    key_matrix,
    value_matrix,
    query_bias,
    value_bias,
    output_matrix,
    b_out,
    gain_one,
    shift_one,
    gain_two,
    shift_two,
    expand_weight,
    expand_bias,
    contract_weight,
    b_down,
    grad_out,
):
    slots, rows, width = cells.shape
    n_dp, n_mp = lax.axis_size("dp"), lax.axis_size("mp")
    d, z = lax.axis_index("dp"), lax.axis_index("mp")
    per = n_mp // slots
    core = d % per
    tokens = slots * rows
    part = width // n_dp
    hw = query_matrix.shape[1]
    turns = moves(n_dp, n_mp, slots)

    def bring(x):
        got = [
            lax.ppermute(
                lax.dynamic_index_in_dim(x, (t + z) % slots, 0, False), ("dp", "mp"), turns[t]
            )
            for t in range(slots)
        ]
        even = z % slots == 0
        return jnp.concatenate(
            [jnp.where(even, got[0], got[1]), jnp.where(even, got[1], got[0])], 0
        )

    def give_back(x):
        x = x.reshape(slots, rows, width)
        got = [
            lax.ppermute(
                lax.dynamic_index_in_dim(x, (t + z) % slots, 0, False),
                ("dp", "mp"),
                [(b, a) for a, b in turns[t]],
            )
            for t in range(slots)
        ]
        even = z % slots == 0
        return jnp.stack(
            [jnp.where(even, got[0], got[1]), jnp.where(even, got[1], got[0])], 0
        )

    mine = bring(cells)
    attn_own = jnp.concatenate(
        [query_matrix, key_matrix, value_matrix, output_matrix.T], 1
    )
    first = d * part

    def piece_of(w):
        return lax.dynamic_slice_in_dim(w, first, part, 0)

    half = attn_own.shape[1] // 2
    a_piece = piece_of(attn_own)
    a_left = gather(a_piece[:, :half], False)
    a_right = gather(a_piece[:, half:], True)
    u_held = gather(piece_of(expand_weight), False)
    d_held = gather(piece_of(contract_weight), True)
    grad_rows = bring(grad_out)
    small = jnp.concatenate([query_bias, value_bias, expand_bias])
    small = [small] + [shift(small, n_mp - r) for r in range(1, n_mp)]
    both = cross(lengths, 0)
    length_all = jnp.where(core == 0, jnp.concatenate([lengths, both]), jnp.concatenate([both, lengths]))
    length = lax.dynamic_index_in_dim(length_all, z, 0, False)

    attn_w = [
        jnp.concatenate([a, b], 1)
        for a, b in zip(
            assemble(a_left, attn_own[:, :half], d), assemble(a_right, attn_own[:, half:], d)
        )
    ]
    up_w = assemble(u_held, expand_weight, d)
    down_w = assemble(d_held, contract_weight, d)

    position = core * tokens + jnp.arange(tokens)
    keep = (position < length).astype(F32)[:, None]
    sib_position = (per - 1 - core) * tokens + jnp.arange(tokens)
    allowed = jnp.concatenate([position, sib_position]) < length

    x = mine.astype(F32)
    rows_one, unit_one, inv_one = layer_norm(x, gain_one, shift_one)
    rows_one = rows_one.astype(BF)
    kept = []
    attention = jnp.zeros((tokens, width), F32)
    for r in range(n_mp):
        w = attn_w[r]
        q = (dot(rows_one, w[:, :hw], 1, 0) + small[r][:hw]).astype(BF)
        k = dot(rows_one, w[:, hw : 2 * hw], 1, 0).astype(BF)
        v = (dot(rows_one, w[:, 2 * hw : 3 * hw], 1, 0) + small[r][hw : 2 * hw]).astype(BF)
        k = jnp.concatenate([k, cross(k, 0)], 0)
        v = jnp.concatenate([v, cross(v, 0)], 0)
        mixed, p = attend(q, k, v, allowed)
        kept.append((q, k, v, mixed, p))
        attention = attention + dot(mixed, w[:, 3 * hw :], 1, 1)
    middle = x + attention + b_out
    rows_two, unit_two, inv_two = layer_norm(middle, gain_two, shift_two)
    rows_two = rows_two.astype(BF)
    g = keep * grad_rows.astype(F32)
    gz = g.astype(BF)

    order = jnp.arange(0, n_dp, 2) ^ d

    def chosen(v):
        return jnp.take(v.reshape(v.shape[0], n_dp, part), order, axis=1).reshape(v.shape[0], -1)

    def other(v):
        return jnp.take(v.reshape(v.shape[0], n_dp, part), order ^ 1, axis=1).reshape(v.shape[0], -1)

    def both_cores(v):
        return jnp.concatenate([chosen(v), cross(other(v), 0)], 0)

    def weight_grad(left, right, flip):
        right = jnp.concatenate([right, cross(right, 0)], 0)
        return weight_grad_all(left, right, flip)

    def weight_grad_all(left, right, flip):
        got = dot(left, right, 0, 0).astype(BF).reshape(-1, part, right.shape[1])
        return scatter({2 * i: got[i] for i in range(got.shape[0])}, flip)

    def finish(pieces):
        total = pieces[0].astype(F32)
        for r in range(1, n_mp):
            total = total + shift(pieces[r], r).astype(F32)
        return total

    two_both = both_cores(rows_two)
    gz_both = both_cores(gz)
    result = middle + b_down
    e2 = jnp.zeros((tokens, width), F32)
    up_parts, down_parts, b_up = [], [], []
    for r in range(n_mp):
        upper = dot(rows_two, up_w[r], 1, 0) + small[r][2 * hw :]
        hidden, slope = gelu_pair(upper)
        hidden = hidden.astype(BF)
        result = result + dot(hidden, down_w[r], 1, 0)
        d_upper = (dot(gz, down_w[r], 1, 1) * slope).astype(BF)
        e2 = e2 + dot(d_upper, up_w[r], 1, 1)
        up_parts.append(weight_grad(two_both, d_upper, False))
        down_parts.append(weight_grad(gz_both, hidden, True))
        b_up.append(jnp.sum(d_upper.astype(F32), 0))
    out_cells = give_back((keep * result).astype(BF))
    grad_up = finish(up_parts)
    grad_down = finish(down_parts).T

    d_middle = g + norm_back(e2, unit_two, inv_two, gain_two)
    gm = d_middle.astype(BF)
    gm_both = both_cores(gm)
    one_both = both_cores(rows_one)
    e1 = jnp.zeros((tokens, width), F32)
    a_parts, b_q, b_v = [], [], []
    for r in range(n_mp):
        q, k, v, mixed, p = kept[r]
        w = attn_w[r]
        d_mixed = dot(gm, w[:, 3 * hw :], 1, 0).astype(BF)
        dq, dk, dv = attend_back(q, k, v, p, mixed, d_mixed)
        dk_all = (dk.astype(F32) + jnp.roll(cross(dk, 0), tokens, 0).astype(F32)).astype(BF)
        dv_all = (dv.astype(F32) + jnp.roll(cross(dv, 0), tokens, 0).astype(F32)).astype(BF)
        dq_all = jnp.concatenate([dq, cross(dq, 0)], 0)
        e1 = (
            e1
            + dot(dq, w[:, :hw], 1, 1)
            + dot(dk_all[:tokens], w[:, hw : 2 * hw], 1, 1)
            + dot(dv_all[:tokens], w[:, 2 * hw : 3 * hw], 1, 1)
        )
        b_q.append(jnp.sum(dq.astype(F32), 0))
        b_v.append(jnp.sum(dv_all[:tokens].astype(F32), 0))
        qkv_part = weight_grad_all(one_both, jnp.concatenate([dq_all, dk_all, dv_all], 1), r % 2 == 1)
        o_part = weight_grad(gm_both, mixed, r % 2 == 0)
        a_parts.append(jnp.concatenate([qkv_part, o_part], 1))
    d_cells = d_middle + norm_back(e1, unit_one, inv_one, gain_one)
    grad_cells = give_back(d_cells.astype(BF)).astype(F32)
    grad_attn = finish(a_parts)

    split_mp = [jnp.stack(b_q).reshape(n_mp, n_dp, -1), jnp.stack(b_v).reshape(n_mp, n_dp, -1), jnp.stack(b_up).reshape(n_mp, n_dp, -1)]
    sums = [
        jnp.sum(d_middle, 0),
        jnp.sum(e1 * unit_one, 0),
        jnp.sum(e1, 0),
        jnp.sum(e2 * unit_two, 0),
        jnp.sum(e2, 0),
        jnp.sum(g, 0),
    ]
    split_dp = [jnp.roll(jnp.swapaxes(s.reshape(n_dp, n_mp, -1), 0, 1), -z, 0) for s in sums]
    packed = jnp.concatenate(split_mp + split_dp, 2)
    packed = jnp.take(packed, jnp.arange(n_dp) ^ d, axis=1)
    packed = packed[:, 0::2] + cross(packed[:, 1::2], 0)
    packed = scatter({2 * i: packed[:, i] for i in range(packed.shape[1])}, False)
    vec = packed[0]
    for r in range(1, n_mp):
        vec = vec + shift(packed[r], r)
    nq = split_mp[0].shape[2]
    nu = split_mp[2].shape[2]
    ns = split_dp[0].shape[2]
    vq, vv, vu = vec[:nq], vec[nq : 2 * nq], vec[2 * nq : 2 * nq + nu]
    rest = [vec[2 * nq + nu + i * ns : 2 * nq + nu + (i + 1) * ns] for i in range(6)]
    return (
        out_cells,
        grad_cells,
        grad_attn[:, :hw],
        grad_attn[:, hw : 2 * hw],
        grad_attn[:, 2 * hw : 3 * hw],
        vq,
        vv,
        grad_attn[:, 3 * hw :].T,
        rest[0],
        rest[1],
        rest[2],
        rest[3],
        rest[4],
        grad_up,
        vu,
        grad_down,
        rest[5],
    )


def solution(mesh):
    return jax.shard_map(
        body,
        mesh=mesh,
        in_specs=(
            P("dp", "mp", None),
            P("dp"),
            P(None, "mp"),
            P(None, "mp"),
            P(None, "mp"),
            P("mp"),
            P("mp"),
            P("mp", None),
            P(),
            P(),
            P(),
            P(),
            P(),
            P(None, "mp"),
            P("mp"),
            P("mp", None),
            P(),
            P("dp", "mp", None),
        ),
        out_specs=(
            P("dp", "mp", None),
            P("dp", "mp", None),
            P("dp", "mp"),
            P("dp", "mp"),
            P("dp", "mp"),
            P(("mp", "dp")),
            P(("mp", "dp")),
            P("mp", "dp"),
            P(("dp", "mp")),
            P(("dp", "mp")),
            P(("dp", "mp")),
            P(("dp", "mp")),
            P(("dp", "mp")),
            P("dp", "mp"),
            P(("mp", "dp")),
            P("mp", "dp"),
            P(("dp", "mp")),
        ),
        check_vma=False,
    )
```

time: 1550 us -> 874 us (0.56)
  waiting for transfers between devices: 1210 us -> 233 us
  starting transfers between devices: 0.89 us -> 150 us
  local copies, waits for them, and re-layouts: 30.2 us -> 157 us
  other arithmetic: 74.9 us -> 132 us
  blocking collectives: 53.4 us -> 0 us
  matrix products: 163 us -> 193 us
    psum x4 -> x0, waiting for transfers between devices: 849 us -> none  [the longest x1 289 us: body(): attention_total = lax.psum(attention_piece, 'mp')]
    ppermute x0 -> x135, waiting for transfers between devices: none -> 233 us  [the longest x100 104 us: cross(): return lax.ppermute(x, 'dp', [(i, i ^ 1 << bit) for i in range(n)])]
    reduce_scatter x6 -> x0, waiting for transfers between devices: 217 us -> none  [the longest x1 55.1 us: body(): lax.psum_scatter(grad_w_down_local, 'dp', scatter_dimension=1, tiled=True)]
    ppermute x0 -> x135, starting transfers between devices: none -> 150 us  [the longest x100 82.7 us: cross(): return lax.ppermute(x, 'dp', [(i, i ^ 1 << bit) for i in range(n)])]
    all_gather x2 -> x0, waiting for transfers between devices: 140 us -> none  [the longest x1 79.7 us: body(): lax.all_gather(cells, 'mp', axis=1, tiled=True)]
    unnamed x2 -> x0, blocking collectives: 53.4 us -> none
    convert_element_type x4 -> x54, other arithmetic: 20.2 us -> 64 us  [the longest x4 20 us: attend_back(): ds = (pf * (dp - total)).astype(BF)]
    gather x0 -> x13, local copies, waits for them, and re-layouts: none -> 40.8 us  [the longest x4 21.3 us: assemble(): placed = jnp.take(stack, order, axis=0)]
  transfers between devices with their start and end apart: 12 -> 135, of which waited for: 12 -> 48; matrix products, arithmetic and copies ran while one was open for 12% -> 53% of each run, Pallas kernels for 0% -> 0%
where the time goes in v1:
time: 874 us; the launch traced here: 868 us
  waiting for transfers between devices  233 us (27%)
  matrix products  193 us (22%)
  local copies, waits for them, and re-layouts  157 us (18%)
  starting transfers between devices  150 us (17%)
  other arithmetic  132 us (15%)
    dot_general x64, matrix products, dot(): lax.dot_general(a, b, (((ca,), (cb,)), ((), ())), preferred_element_type=...  113 us
    ppermute x100, waiting for transfers between devices, cross(): return lax.ppermute(x, 'dp', [(i, i ^ 1 << bit) for i in range(n)])  104 us
    ppermute x27, waiting for transfers between devices, shift(): return lax.ppermute(x, 'mp', [(i, (i + by) % n) for i in range(n)])  84.8 us
    ppermute x100, starting transfers between devices, cross(): return lax.ppermute(x, 'dp', [(i, i ^ 1 << bit) for i in range(n)])  82.7 us
    unnamed x509, local copies, waits for them, and re-layouts  52.4 us
    ppermute x27, starting transfers between devices, shift(): return lax.ppermute(x, 'mp', [(i, (i + by) % n) for i in range(n)])  28.8 us
    sub x4, matrix products, attend(): e = jnp.exp(s - jnp.max(s, -1, keepdims=True))  28.1 us
    ppermute x4, waiting for transfers between devices, give_back(): lax.ppermute(lax.dynamic_index_in_dim(x, (t + z) % slots, 0, False), ('dp...  26.7 us
  transfers between devices with their start and end apart: 135, of which 48 were waited for; matrix products, arithmetic and copies ran while one was open for 53% of the time, Pallas kernels for 0%

profile of v1, /device:TPU:9, one launch (start us, length us, event | category | flops | bytes accessed | tf_op | source)
XLA Modules:
  0.0 868.4 jit_solution(13803881235717295576)
XLA Ops:
  45.1 11.4 %collective-permute-done.19 = bf16[128,512]{1,0:T(8,128)(2,1)S(1)} collective-permute-done((bf16[128,512]{1,0:T(8,128)(2,1)}, bf16[128,512]{1,0:T(8,128)(2,1)S(1)}, u32[]{:S(2)}, u32[]{:S(2)}) %collective-permute-start.19) | collective-permute-done | bytes 131104 | tf_op jit(solution)/shard_map/ppermute | solution.py:23
  60.7 12.7 %collective-permute-done.35 = bf16[128,1024]{1,0:T(8,128)(2,1)S(1)} collective-permute-done((bf16[128,1024]{1,0:T(8,128)(2,1)}, bf16[128,1024]{1,0:T(8,128)(2,1)S(1)}, u32[]{:S(2)}, u32[]{:S(2)}) %collective-permute-start.35) | collective-permute-done | bytes 262176 | tf_op jit(solution)/shard_map/ppermute | solution.py:23
  73.4 5.4 collective-permute-start.1
  79.0 3.8 collective-permute-start.2
  84.7 5.8 collective-permute-done.44
  92.7 13.9 %collective-permute-start.57 = (bf16[256,1024]{1,0:T(8,128)(2,1)}, bf16[256,1024]{1,0:T(8,128)(2,1)S(1)}, u32[]{:S(2)}, u32[]{:S(2)}) collective-permute-start(bf16[256,1024]{1,0:T(8,128)(2,1)} %get-tuple-element.122), channel_id=1, source_target_pairs={{0,1},{1,0},{2,5},{3,4},{4,3},{5,2},{6,7},{7,6},{8,9},{9,8},{10,13... | collective-permute-start | bytes 1572872 | tf_op jit(solution)/shard_map/ppermute | solution.py:161
  110.8 7.6 collective-permute-done.1
  119.6 4.4 collective-permute-done.2
  129.9 5.4 collective-permute-done.57
  166.1 7.0 fusion.379
  173.1 4.6 divide_convert_fusion.3
  192.1 7.0 collective-permute-done.13
  202.9 9.3 %collective-permute-done.25 = bf16[3,128,512]{2,1,0:T(8,128)(2,1)S(1)} collective-permute-done((bf16[3,128,512]{2,1,0:T(8,128)(2,1)}, bf16[3,128,512]{2,1,0:T(8,128)(2,1)S(1)}, u32[]{:S(2)}, u32[]{:S(2)}) %collective-permute-start.25) | collective-permute-done | bytes 393248 | tf_op jit(solution)/shard_map/ppermute | solution.py:18
  221.2 9.2 %collective-permute-done.48 = bf16[3,128,1024]{2,1,0:T(8,128)(2,1)S(1)} collective-permute-done((bf16[3,128,1024]{2,1,0:T(8,128)(2,1)}, bf16[3,128,1024]{2,1,0:T(8,128)(2,1)S(1)}, u32[]{:S(2)}, u32[]{:S(2)}) %collective-permute-start.48) | collective-permute-done | bytes 786464 | tf_op jit(solution)/shard_map/ppermute | solution.py:18
  233.0 4.3 gather_fusion.1
  239.1 4.3 gather_fusion.2
  243.3 3.5 select_bitcast_fusion.2
  271.0 7.0 fusion.380
  278.0 4.2 divide_convert_fusion.2
  284.3 7.1 fusion.378
  291.4 5.5 divide_convert_fusion.1
  306.8 4.5 convolution_convert_fusion.17
  319.1 7.0 fusion.377
  326.1 4.4 divide_convert_fusion
  339.7 3.6 convert_reduce_fusion.4
  350.1 4.0 fusion.386
  354.1 3.9 fusion.383
  368.9 8.1 collective-permute-done.52
  384.2 6.3 gather_fusion.3
  391.5 6.4 gather_fusion.4
  397.9 10.3 %select_bitcast_fusion = (bf16[3,8,128,1024]{3,2,0,1:T(8,128)(2,1)}, bf16[3,8,128,1024]{3,2,0,1:T(8,128)(2,1)}) fusion(bf16[8,3,128,1024]{3,2,1,0:T(8,128)(2,1)} %gather_fusion.4, pred[8]{0:T(512)(128)(4,1)S(1)} %copy-done.199, bf16[8,3,128,1024]{3,2,1,0:T(8,128)(2,1)} %gather_fusion.3), kind=kLoop, calls=%fused_computation.49 | loop fusion | flops 6291456 | bytes 25165832 | tf_op jit(solution)/shard_map/transpose | solution.py:60
  408.1 5.9 fusion.360
  447.8 4.6 fusion.4
  454.1 4.6 fusion.6
  460.4 4.7 fusion.8
  466.7 4.6 fusion.10
  471.4 4.5 fusion.5
  479.1 4.3 fusion.7
  487.2 4.2 fusion.9
  500.6 6.9 fusion.11
  516.0 3.3 fusion.384
  560.5 3.5 fusion.41
  610.8 5.4 collective-permute-done.54
  616.2 12.8 %collective-permute-done.55 = bf16[256,1024]{1,0:T(8,128)(2,1)S(1)} collective-permute-done((bf16[256,1024]{1,0:T(8,128)(2,1)S(1)}, bf16[256,1024]{1,0:T(8,128)(2,1)S(1)}, u32[]{:S(2)}, u32[]{:S(2)}) %collective-permute-start.55) | collective-permute-done | bytes 524320 | tf_op jit(solution)/shard_map/ppermute | solution.py:174
  645.0 5.3 collective-permute-done.80
  674.2 4.0 collective-permute-done.77
  680.3 12.2 %collective-permute-start.107 = (bf16[512,1024]{1,0:T(8,128)(2,1)S(1)}, bf16[512,1024]{1,0:T(8,128)(2,1)S(1)}, u32[]{:S(2)}, u32[]{:S(2)}) collective-permute-start(bf16[512,1024]{1,0:T(8,128)(2,1)S(1)} %copy-done.228), channel_id=1, source_target_pairs={{0,4},{4,0},{8,12},{12,8},{16,20},{20,16},{24,28},{28,24},{1,5},{5... | collective-permute-start | bytes 3145736 | tf_op jit(solution)/shard_map/ppermute | solution.py:18
  692.6 6.0 collective-permute-start.111
  708.4 4.6 collective-permute-start.66
  714.4 3.7 collective-permute-start.67
  730.2 8.5 collective-permute-done.67
  744.9 13.3 %collective-permute-done.82 = bf16[128,1024]{1,0:T(8,128)(2,1)S(1)} collective-permute-done((bf16[128,1024]{1,0:T(8,128)(2,1)S(1)}, bf16[128,1024]{1,0:T(8,128)(2,1)S(1)}, u32[]{:S(2)}, u32[]{:S(2)}) %collective-permute-start.82) | collective-permute-done | bytes 262176 | tf_op jit(solution)/shard_map/ppermute | solution.py:23
  759.0 4.9 collective-permute-done.89
  772.8 8.9 %collective-permute-done.132 = bf16[2,128,1024]{2,1,0:T(8,128)(2,1)} collective-permute-done((bf16[2,128,1024]{2,1,0:T(8,128)(2,1)}, bf16[2,128,1024]{2,1,0:T(8,128)(2,1)}, u32[]{:S(2)}, u32[]{:S(2)}) %collective-permute-start.132) | collective-permute-done | bytes 524320 | tf_op jit(solution)/shard_map/ppermute | solution.py:18
  785.2 3.2 collective-permute-done.112
  789.7 9.9 %collective-permute-done.116 = bf16[2,128,1024]{2,1,0:T(8,128)(2,1)S(1)} collective-permute-done((bf16[2,128,1024]{2,1,0:T(8,128)(2,1)}, bf16[2,128,1024]{2,1,0:T(8,128)(2,1)S(1)}, u32[]{:S(2)}, u32[]{:S(2)}) %collective-permute-start.116) | collective-permute-done | bytes 524320 | tf_op jit(solution)/shard_map/ppermute | solution.py:18
  800.3 5.0 collective-permute-done.125
  807.0 3.9 collective-permute-done.129
  812.6 3.9 collective-permute-done.133
  817.6 3.2 collective-permute-start.130
  828.3 9.9 %collective-permute-done.130 = bf16[128,1024]{1,0:T(8,128)(2,1)S(1)} collective-permute-done((bf16[128,1024]{1,0:T(8,128)(2,1)S(1)}, bf16[128,1024]{1,0:T(8,128)(2,1)S(1)}, u32[]{:S(2)}, u32[]{:S(2)}) %collective-permute-start.130) | collective-permute-done | bytes 262176 | tf_op jit(solution)/shard_map/ppermute | solution.py:23
  840.9 13.6 %collective-permute-done.134 = bf16[128,1024]{1,0:T(8,128)(2,1)S(1)} collective-permute-done((bf16[128,1024]{1,0:T(8,128)(2,1)S(1)}, bf16[128,1024]{1,0:T(8,128)(2,1)S(1)}, u32[]{:S(2)}, u32[]{:S(2)}) %collective-permute-start.134) | collective-permute-done | bytes 262176 | tf_op jit(solution)/shard_map/ppermute | solution.py:23
  857.0 3.9 collective-permute-done.114
  860.8 5.0 collective-permute-done.118
  (1051 shorter events, 459.8 us)
Async XLA Ops:
  3.8 33.3 %collective-permute-start.6 = (bf16[128,512]{1,0:T(8,128)(2,1)}, bf16[128,512]{1,0:T(8,128)(2,1)S(1)}, u32[]{:S(2)}, u32[]{:S(2)}) collective-permute-start(bf16[128,512]{1,0:T(8,128)(2,1)} %get-tuple-element.168), channel_id=1, source_target_pairs={{0,2},{1,3},{2,0},{3,1},{4,6},{5,7},{6,4},{7,5},{8,10},{9,11},{10,... | collective-permute-start | bytes 393224 | tf_op jit(solution)/shard_map/ppermute | solution.py:23
  6.1 32.3 %collective-permute-start.7 = (bf16[128,512]{1,0:T(8,128)(2,1)}, bf16[128,512]{1,0:T(8,128)(2,1)S(1)}, u32[]{:S(2)}, u32[]{:S(2)}) collective-permute-start(bf16[128,512]{1,0:T(8,128)(2,1)} %get-tuple-element.168), channel_id=1, source_target_pairs={{0,1},{1,2},{2,3},{3,0},{4,5},{5,6},{6,7},{7,4},{8,9},{9,10},{10,1... | collective-permute-start | bytes 393224 | tf_op jit(solution)/shard_map/ppermute | solution.py:23
  6.1 32.5 %collective-permute-start.5 = (bf16[128,512]{1,0:T(8,128)(2,1)}, bf16[128,512]{1,0:T(8,128)(2,1)S(1)}, u32[]{:S(2)}, u32[]{:S(2)}) collective-permute-start(bf16[128,512]{1,0:T(8,128)(2,1)} %get-tuple-element.168), channel_id=1, source_target_pairs={{0,3},{1,0},{2,1},{3,2},{4,7},{5,4},{6,5},{7,6},{8,11},{9,8},{10,9... | collective-permute-start | bytes 393224 | tf_op jit(solution)/shard_map/ppermute | solution.py:23
  38.4 22.3 %collective-permute-start.34 = (bf16[128,1024]{1,0:T(8,128)(2,1)}, bf16[128,1024]{1,0:T(8,128)(2,1)S(1)}, u32[]{:S(2)}, u32[]{:S(2)}) collective-permute-start(bf16[128,1024]{1,0:T(8,128)(2,1)} %constant_dynamic-slice_fusion.1), channel_id=1, source_target_pairs={{0,3},{1,0},{2,1},{3,2},{4,7},{5,4},{6,5},{7,6},{8,11},{9,8},{10,9... | collective-permute-start | bytes 786440 | tf_op jit(solution)/shard_map/ppermute | solution.py:23
  38.6 34.8 %collective-permute-start.35 = (bf16[128,1024]{1,0:T(8,128)(2,1)}, bf16[128,1024]{1,0:T(8,128)(2,1)S(1)}, u32[]{:S(2)}, u32[]{:S(2)}) collective-permute-start(bf16[128,1024]{1,0:T(8,128)(2,1)} %constant_dynamic-slice_fusion.1), channel_id=1, source_target_pairs={{0,2},{1,3},{2,0},{3,1},{4,6},{5,7},{6,4},{7,5},{8,10},{9,11},{10,... | collective-permute-start | bytes 786440 | tf_op jit(solution)/shard_map/ppermute | solution.py:23
  40.4 38.6 %collective-permute-start.36 = (bf16[128,1024]{1,0:T(8,128)(2,1)}, bf16[128,1024]{1,0:T(8,128)(2,1)S(1)}, u32[]{:S(2)}, u32[]{:S(2)}) collective-permute-start(bf16[128,1024]{1,0:T(8,128)(2,1)} %constant_dynamic-slice_fusion.1), channel_id=1, source_target_pairs={{0,1},{1,2},{2,3},{3,0},{4,5},{5,6},{6,7},{7,4},{8,9},{9,10},{10,1... | collective-permute-start | bytes 786440 | tf_op jit(solution)/shard_map/ppermute | solution.py:23
  43.2 47.2 %collective-permute-start.44 = (bf16[128,1024]{1,0:T(8,128)(2,1)}, bf16[128,1024]{1,0:T(8,128)(2,1)S(1)}, u32[]{:S(2)}, u32[]{:S(2)}) collective-permute-start(bf16[128,1024]{1,0:T(8,128)(2,1)} %constant_dynamic-slice_fusion), channel_id=1, source_target_pairs={{0,3},{1,0},{2,1},{3,2},{4,7},{5,4},{6,5},{7,6},{8,11},{9,8},{10,9... | collective-permute-start | bytes 786440 | tf_op jit(solution)/shard_map/ppermute | solution.py:23
  56.5 36.2 %collective-permute-start.45 = (bf16[128,1024]{1,0:T(8,128)(2,1)}, bf16[128,1024]{1,0:T(8,128)(2,1)S(1)}, u32[]{:S(2)}, u32[]{:S(2)}) collective-permute-start(bf16[128,1024]{1,0:T(8,128)(2,1)} %constant_dynamic-slice_fusion), channel_id=1, source_target_pairs={{0,2},{1,3},{2,0},{3,1},{4,6},{5,7},{6,4},{7,5},{8,10},{9,11},{10,... | collective-permute-start | bytes 786440 | tf_op jit(solution)/shard_map/ppermute | solution.py:23
  60.7 46.3 %collective-permute-start.46 = (bf16[128,1024]{1,0:T(8,128)(2,1)S(1)}, bf16[128,1024]{1,0:T(8,128)(2,1)S(1)}, u32[]{:S(2)}, u32[]{:S(2)}) collective-permute-start(bf16[128,1024]{1,0:T(8,128)(2,1)S(1)} %copy-done.181), channel_id=1, source_target_pairs={{0,1},{1,2},{2,3},{3,0},{4,5},{5,6},{6,7},{7,4},{8,9},{9,10},{10,1... | collective-permute-start | bytes 786440 | tf_op jit(solution)/shard_map/ppermute | solution.py:23
  73.4 45.0 %collective-permute-start.1 = (bf16[256,1024]{1,0:T(8,128)(2,1)S(1)}, bf16[256,1024]{1,0:T(8,128)(2,1)S(1)}, u32[]{:S(2)}, u32[]{:S(2)}) collective-permute-start(bf16[256,1024]{1,0:T(8,128)(2,1)S(1)} %copy-done.176), channel_id=1, source_target_pairs={{0,0},{1,1},{2,4},{3,5},{4,2},{5,3},{6,6},{7,7},{8,8},{9,9},{10,12... | collective-permute-start | bytes 1572872 | tf_op jit(solution)/shard_map/ppermute | solution.py:161
  79.0 45.0 %collective-permute-start.2 = (bf16[256,1024]{1,0:T(8,128)(2,1)S(1)}, bf16[256,1024]{1,0:T(8,128)(2,1)S(1)}, u32[]{:S(2)}, u32[]{:S(2)}) collective-permute-start(bf16[256,1024]{1,0:T(8,128)(2,1)S(1)} %copy-done.175), channel_id=1, source_target_pairs={{0,1},{1,0},{2,5},{3,4},{4,3},{5,2},{6,7},{7,6},{8,9},{9,8},{10,13... | collective-permute-start | bytes 1572872 | tf_op jit(solution)/shard_map/ppermute | solution.py:161
  90.5 39.4 %collective-permute-start.56 = (bf16[256,1024]{1,0:T(8,128)(2,1)}, bf16[256,1024]{1,0:T(8,128)(2,1)S(1)}, u32[]{:S(2)}, u32[]{:S(2)}) collective-permute-start(bf16[256,1024]{1,0:T(8,128)(2,1)} %get-tuple-element.121), channel_id=1, source_target_pairs={{0,0},{1,1},{2,4},{3,5},{4,2},{5,3},{6,6},{7,7},{8,8},{9,9},{10,12... | collective-permute-start | bytes 1572872 | tf_op jit(solution)/shard_map/ppermute | solution.py:161
  92.7 42.7 %collective-permute-start.57 = (bf16[256,1024]{1,0:T(8,128)(2,1)}, bf16[256,1024]{1,0:T(8,128)(2,1)S(1)}, u32[]{:S(2)}, u32[]{:S(2)}) collective-permute-start(bf16[256,1024]{1,0:T(8,128)(2,1)} %get-tuple-element.122), channel_id=1, source_target_pairs={{0,1},{1,0},{2,5},{3,4},{4,3},{5,2},{6,7},{7,6},{8,9},{9,8},{10,13... | collective-permute-start | bytes 1572872 | tf_op jit(solution)/shard_map/ppermute | solution.py:161
  107.0 33.5 %collective-permute-start.8 = (bf16[3,128,512]{2,1,0:T(8,128)(2,1)}, bf16[3,128,512]{2,1,0:T(8,128)(2,1)S(1)}, u32[]{:S(2)}, u32[]{:S(2)}) collective-permute-start(bf16[3,128,512]{2,1,0:T(8,128)(2,1)} %pad_maximum_fusion.25), channel_id=1, source_target_pairs={{0,4},{4,0},{8,12},{12,8},{16,20},{20,16},{24,28},{28,24},{1,5},{5... | collective-permute-start | bytes 1179656 | tf_op jit(solution)/shard_map/ppermute | solution.py:18
  118.4 24.1 %collective-permute-start.9 = (bf16[3,128,512]{2,1,0:T(8,128)(2,1)}, bf16[3,128,512]{2,1,0:T(8,128)(2,1)S(1)}, u32[]{:S(2)}, u32[]{:S(2)}) collective-permute-start(bf16[3,128,512]{2,1,0:T(8,128)(2,1)} %pad_maximum_fusion.25), channel_id=1, source_target_pairs={{0,8},{4,12},{8,0},{12,4},{16,24},{20,28},{24,16},{28,20},{1,9},{5... | collective-permute-start | bytes 1179656 | tf_op jit(solution)/shard_map/ppermute | solution.py:18
  124.0 60.6 %collective-permute-start.11 = (bf16[3,128,512]{2,1,0:T(8,128)(2,1)}, bf16[3,128,512]{2,1,0:T(8,128)(2,1)}, u32[]{:S(2)}, u32[]{:S(2)}) collective-permute-start(bf16[3,128,512]{2,1,0:T(8,128)(2,1)} %pad_maximum_fusion.25), channel_id=1, source_target_pairs={{0,16},{4,20},{8,24},{12,28},{16,0},{20,4},{24,8},{28,12},{1,17},{... | collective-permute-start | bytes 1179656 | tf_op jit(solution)/shard_map/ppermute | solution.py:18
  140.5 47.5 %collective-permute-start.23 = (bf16[3,128,512]{2,1,0:T(8,128)(2,1)}, bf16[3,128,512]{2,1,0:T(8,128)(2,1)}, u32[]{:S(2)}, u32[]{:S(2)}) collective-permute-start(bf16[3,128,512]{2,1,0:T(8,128)(2,1)} %pad_maximum_fusion.26), channel_id=1, source_target_pairs={{0,16},{4,20},{8,24},{12,28},{16,0},{20,4},{24,8},{28,12},{1,17},{... | collective-permute-start | bytes 1179656 | tf_op jit(solution)/shard_map/ppermute | solution.py:18
  142.5 71.6 %collective-permute-start.37 = (bf16[3,128,1024]{2,1,0:T(8,128)(2,1)}, bf16[3,128,1024]{2,1,0:T(8,128)(2,1)}, u32[]{:S(2)}, u32[]{:S(2)}) collective-permute-start(bf16[3,128,1024]{2,1,0:T(8,128)(2,1)} %pad_maximum_fusion.7), channel_id=1, source_target_pairs={{0,4},{4,0},{8,12},{12,8},{16,20},{20,16},{24,28},{28,24},{1,5},{5... | collective-permute-start | bytes 2359304 | tf_op jit(solution)/shard_map/ppermute | solution.py:18
  157.7 58.8 %collective-permute-start.38 = (bf16[3,128,1024]{2,1,0:T(8,128)(2,1)}, bf16[3,128,1024]{2,1,0:T(8,128)(2,1)}, u32[]{:S(2)}, u32[]{:S(2)}) collective-permute-start(bf16[3,128,1024]{2,1,0:T(8,128)(2,1)} %pad_maximum_fusion.7), channel_id=1, source_target_pairs={{0,8},{4,12},{8,0},{12,4},{16,24},{20,28},{24,16},{28,20},{1,9},{5... | collective-permute-start | bytes 2359304 | tf_op jit(solution)/shard_map/ppermute | solution.py:18
  161.9 20.7 %collective-permute-start.10 = (bf16[3,128,512]{2,1,0:T(8,128)(2,1)}, bf16[3,128,512]{2,1,0:T(8,128)(2,1)}, u32[]{:S(2)}, u32[]{:S(2)}) collective-permute-start(bf16[3,128,512]{2,1,0:T(8,128)(2,1)} %copy-done.180), channel_id=1, source_target_pairs={{0,4},{4,0},{8,12},{12,8},{16,20},{20,16},{24,28},{28,24},{1,5},{5... | collective-permute-start | bytes 1179656 | tf_op jit(solution)/shard_map/ppermute | solution.py:18
  184.7 129.6 %collective-permute-start.40 = (bf16[3,128,1024]{2,1,0:T(8,128)(2,1)}, bf16[3,128,1024]{2,1,0:T(8,128)(2,1)}, u32[]{:S(2)}, u32[]{:S(2)}) collective-permute-start(bf16[3,128,1024]{2,1,0:T(8,128)(2,1)} %pad_maximum_fusion.7), channel_id=1, source_target_pairs={{0,16},{4,20},{8,24},{12,28},{16,0},{20,4},{24,8},{28,12},{1,17},{... | collective-permute-start | bytes 2359304 | tf_op jit(solution)/shard_map/ppermute | solution.py:18
  214.2 143.9 %collective-permute-start.50 = (bf16[3,128,1024]{2,1,0:T(8,128)(2,1)}, bf16[3,128,1024]{2,1,0:T(8,128)(2,1)}, u32[]{:S(2)}, u32[]{:S(2)}) collective-permute-start(bf16[3,128,1024]{2,1,0:T(8,128)(2,1)} %pad_maximum_fusion.8), channel_id=1, source_target_pairs={{0,16},{4,20},{8,24},{12,28},{16,0},{20,4},{24,8},{28,12},{1,17},{... | collective-permute-start | bytes 2359304 | tf_op jit(solution)/shard_map/ppermute | solution.py:18
  259.7 337.6 %collective-permute-start.73 = (bf16[512,256]{0,1:T(8,128)(2,1)}, bf16[512,256]{0,1:T(8,128)(2,1)}, u32[]{:S(2)}, u32[]{:S(2)}) collective-permute-start(bf16[512,256]{0,1:T(8,128)(2,1)} %bitcast.7), channel_id=1, source_target_pairs={{0,4},{4,0},{8,12},{12,8},{16,20},{20,16},{24,28},{28,24},{1,5},{5... | collective-permute-start | bytes 786440 | tf_op jit(solution)/shard_map/ppermute | solution.py:18
  262.6 36.0 %collective-permute-start.29 = (bf16[512,256]{1,0:T(8,128)(2,1)}, bf16[512,256]{1,0:T(8,128)(2,1)}, u32[]{:S(2)}, u32[]{:S(2)}) collective-permute-start(bf16[512,256]{1,0:T(8,128)(2,1)} %add_convert_fusion.13), channel_id=1, source_target_pairs={{0,4},{4,0},{8,12},{12,8},{16,20},{20,16},{24,28},{28,24},{1,5},{5... | collective-permute-start | bytes 786440 | tf_op jit(solution)/shard_map/ppermute | solution.py:18
  267.0 35.9 %collective-permute-start.33 = (bf16[512,256]{1,0:T(8,128)(2,1)}, bf16[512,256]{1,0:T(8,128)(2,1)}, u32[]{:S(2)}, u32[]{:S(2)}) collective-permute-start(bf16[512,256]{1,0:T(8,128)(2,1)} %convolution_convert_fusion.12), channel_id=1, source_target_pairs={{0,4},{4,0},{8,12},{12,8},{16,20},{20,16},{24,28},{28,24},{1,5},{5... | collective-permute-start | bytes 786440 | tf_op jit(solution)/shard_map/ppermute | solution.py:18
  298.6 59.4 %collective-permute-start.39 = (bf16[3,128,1024]{2,1,0:T(8,128)(2,1)}, bf16[3,128,1024]{2,1,0:T(8,128)(2,1)}, u32[]{:S(2)}, u32[]{:S(2)}) collective-permute-start(bf16[3,128,1024]{2,1,0:T(8,128)(2,1)} %collective-permute-done.38), channel_id=1, source_target_pairs={{0,4},{4,0},{8,12},{12,8},{16,20},{20,16},{24,28},{28,24},{1,5},{5... | collective-permute-start | bytes 2359304 | tf_op jit(solution)/shard_map/ppermute | solution.py:18
  314.2 52.1 %collective-permute-start.42 = (bf16[3,128,1024]{2,1,0:T(8,128)(2,1)}, bf16[3,128,1024]{2,1,0:T(8,128)(2,1)}, u32[]{:S(2)}, u32[]{:S(2)}) collective-permute-start(bf16[3,128,1024]{2,1,0:T(8,128)(2,1)} %collective-permute-done.38), channel_id=1, source_target_pairs={{0,16},{4,20},{8,24},{12,28},{16,0},{20,4},{24,8},{28,12},{1,17},{... | collective-permute-start | bytes 2359304 | tf_op jit(solution)/shard_map/ppermute | solution.py:18
  314.4 49.1 %collective-permute-start.41 = (bf16[3,128,1024]{2,1,0:T(8,128)(2,1)}, bf16[3,128,1024]{2,1,0:T(8,128)(2,1)}, u32[]{:S(2)}, u32[]{:S(2)}) collective-permute-start(bf16[3,128,1024]{2,1,0:T(8,128)(2,1)} %collective-permute-done.40), channel_id=1, source_target_pairs={{0,4},{4,0},{8,12},{12,8},{16,20},{20,16},{24,28},{28,24},{1,5},{5... | collective-permute-start | bytes 2359304 | tf_op jit(solution)/shard_map/ppermute | solution.py:18
  366.3 205.2 %collective-permute-start.120 = (bf16[512,1024]{1,0:T(8,128)(2,1)}, bf16[512,1024]{1,0:T(8,128)(2,1)}, u32[]{:S(2)}, u32[]{:S(2)}) collective-permute-start(bf16[512,1024]{1,0:T(8,128)(2,1)} %get-tuple-element.237), channel_id=1, source_target_pairs={{0,4},{4,0},{8,12},{12,8},{16,20},{20,16},{24,28},{28,24},{1,5},{5... | collective-permute-start | bytes 3145736 | tf_op jit(solution)/shard_map/ppermute | solution.py:18
  497.0 67.0 %collective-permute-start.69 = (bf16[512,256]{0,1:T(8,128)(2,1)S(1)}, bf16[512,256]{0,1:T(8,128)(2,1)}, u32[]{:S(2)}, u32[]{:S(2)}) collective-permute-start(bf16[512,256]{0,1:T(8,128)(2,1)S(1)} %bitcast.763), channel_id=1, source_target_pairs={{0,4},{4,0},{8,12},{12,8},{16,20},{20,16},{24,28},{28,24},{1,5},{5... | collective-permute-start | bytes 786440 | tf_op jit(solution)/shard_map/ppermute | solution.py:18
  499.9 67.2 %collective-permute-start.76 = (bf16[512,256]{0,1:T(8,128)(2,1)}, bf16[512,256]{0,1:T(8,128)(2,1)}, u32[]{:S(2)}, u32[]{:S(2)}) collective-permute-start(bf16[512,256]{0,1:T(8,128)(2,1)} %bitcast.102), channel_id=1, source_target_pairs={{0,4},{4,0},{8,12},{12,8},{16,20},{20,16},{24,28},{28,24},{1,5},{5... | collective-permute-start | bytes 786440 | tf_op jit(solution)/shard_map/ppermute | solution.py:18
  509.8 34.9 %collective-permute-start.58 = (bf16[1024,256]{0,1:T(8,128)(2,1)}, bf16[1024,256]{0,1:T(8,128)(2,1)}, u32[]{:S(2)}, u32[]{:S(2)}) collective-permute-start(bf16[1024,256]{0,1:T(8,128)(2,1)} %bitcast.732), channel_id=1, source_target_pairs={{0,4},{4,0},{8,12},{12,8},{16,20},{20,16},{24,28},{28,24},{1,5},{5... | collective-permute-start | bytes 1572872 | tf_op jit(solution)/shard_map/ppermute | solution.py:18
  571.6 29.2 %collective-permute-start.79 = (bf16[512,256]{0,1:T(8,128)(2,1)S(1)}, bf16[512,256]{0,1:T(8,128)(2,1)}, u32[]{:S(2)}, u32[]{:S(2)}) collective-permute-start(bf16[512,256]{0,1:T(8,128)(2,1)S(1)} %bitcast.760), channel_id=1, source_target_pairs={{0,4},{4,0},{8,12},{12,8},{16,20},{20,16},{24,28},{28,24},{1,5},{5... | collective-permute-start | bytes 786440 | tf_op jit(solution)/shard_map/ppermute | solution.py:18
  572.0 32.5 %collective-permute-start.86 = (bf16[512,256]{0,1:T(8,128)(2,1)}, bf16[512,256]{0,1:T(8,128)(2,1)}, u32[]{:S(2)}, u32[]{:S(2)}) collective-permute-start(bf16[512,256]{0,1:T(8,128)(2,1)} %bitcast.46), channel_id=1, source_target_pairs={{0,4},{4,0},{8,12},{12,8},{16,20},{20,16},{24,28},{28,24},{1,5},{5... | collective-permute-start | bytes 786440 | tf_op jit(solution)/shard_map/ppermute | solution.py:18
  580.0 29.0 %collective-permute-start.93 = (bf16[512,256]{0,1:T(8,128)(2,1)}, bf16[512,256]{0,1:T(8,128)(2,1)}, u32[]{:S(2)}, u32[]{:S(2)}) collective-permute-start(bf16[512,256]{0,1:T(8,128)(2,1)} %bitcast.53), channel_id=1, source_target_pairs={{0,4},{4,0},{8,12},{12,8},{16,20},{20,16},{24,28},{28,24},{1,5},{5... | collective-permute-start | bytes 786440 | tf_op jit(solution)/shard_map/ppermute | solution.py:18
  597.3 101.3 %collective-permute-start.123 = (bf16[512,1024]{1,0:T(8,128)(2,1)}, bf16[512,1024]{1,0:T(8,128)(2,1)}, u32[]{:S(2)}, u32[]{:S(2)}) collective-permute-start(bf16[512,1024]{1,0:T(8,128)(2,1)} %get-tuple-element.235), channel_id=1, source_target_pairs={{0,4},{4,0},{8,12},{12,8},{16,20},{20,16},{24,28},{28,24},{1,5},{5... | collective-permute-start | bytes 3145736 | tf_op jit(solution)/shard_map/ppermute | solution.py:18
  597.6 104.0 %collective-permute-start.127 = (bf16[512,1024]{1,0:T(8,128)(2,1)}, bf16[512,1024]{1,0:T(8,128)(2,1)}, u32[]{:S(2)}, u32[]{:S(2)}) collective-permute-start(bf16[512,1024]{1,0:T(8,128)(2,1)} %get-tuple-element.233), channel_id=1, source_target_pairs={{0,4},{4,0},{8,12},{12,8},{16,20},{20,16},{24,28},{28,24},{1,5},{5... | collective-permute-start | bytes 3145736 | tf_op jit(solution)/shard_map/ppermute | solution.py:18
  604.5 24.5 %collective-permute-start.55 = (bf16[256,1024]{1,0:T(8,128)(2,1)S(1)}, bf16[256,1024]{1,0:T(8,128)(2,1)S(1)}, u32[]{:S(2)}, u32[]{:S(2)}) collective-permute-start(bf16[256,1024]{1,0:T(8,128)(2,1)S(1)} %copy-done.169), channel_id=1, source_target_pairs={{1,0},{0,1},{5,2},{4,3},{3,4},{2,5},{7,6},{6,7},{9,8},{8,9},{13,10... | collective-permute-start | bytes 1572872 | tf_op jit(solution)/shard_map/ppermute | solution.py:174
  609.0 21.2 %collective-permute-start.97 = (f32[4,4,384]{2,0,1:T(4,128)S(1)}, f32[4,4,384]{2,0,1:T(4,128)S(1)}, u32[]{:S(2)}, u32[]{:S(2)}) collective-permute-start(f32[4,4,384]{2,0,1:T(4,128)S(1)} %slice.839), channel_id=1, source_target_pairs={{0,4},{4,0},{8,12},{12,8},{16,20},{20,16},{24,28},{28,24},{1,5},{5... | collective-permute-start | bytes 73736 | tf_op jit(solution)/shard_map/ppermute | solution.py:18
  637.9 67.9 %collective-permute-start.131 = (bf16[512,1024]{1,0:T(8,128)(2,1)S(1)}, bf16[512,1024]{1,0:T(8,128)(2,1)S(1)}, u32[]{:S(2)}, u32[]{:S(2)}) collective-permute-start(bf16[512,1024]{1,0:T(8,128)(2,1)S(1)} %copy-done.115), channel_id=1, source_target_pairs={{0,4},{4,0},{8,12},{12,8},{16,20},{20,16},{24,28},{28,24},{1,5},{5... | collective-permute-start | bytes 3145736 | tf_op jit(solution)/shard_map/ppermute | solution.py:18
  639.7 33.2 %collective-permute-start.70 = (bf16[2,128,768]{2,1,0:T(8,128)(2,1)S(1)}, bf16[2,128,768]{2,1,0:T(8,128)(2,1)S(1)}, u32[]{:S(2)}, u32[]{:S(2)}) collective-permute-start(bf16[2,128,768]{2,1,0:T(8,128)(2,1)S(1)} %copy-done.179), channel_id=1, source_target_pairs={{0,8},{4,12},{8,0},{12,4},{16,24},{20,28},{24,16},{28,20},{1,9},{5... | collective-permute-start | bytes 1179656 | tf_op jit(solution)/shard_map/ppermute | solution.py:18
  680.3 28.1 %collective-permute-start.107 = (bf16[512,1024]{1,0:T(8,128)(2,1)S(1)}, bf16[512,1024]{1,0:T(8,128)(2,1)S(1)}, u32[]{:S(2)}, u32[]{:S(2)}) collective-permute-start(bf16[512,1024]{1,0:T(8,128)(2,1)S(1)} %copy-done.228), channel_id=1, source_target_pairs={{0,4},{4,0},{8,12},{12,8},{16,20},{20,16},{24,28},{28,24},{1,5},{5... | collective-permute-start | bytes 3145736 | tf_op jit(solution)/shard_map/ppermute | solution.py:18
  692.6 21.8 %collective-permute-start.111 = (bf16[512,1024]{1,0:T(8,128)(2,1)S(1)}, bf16[512,1024]{1,0:T(8,128)(2,1)S(1)}, u32[]{:S(2)}, u32[]{:S(2)}) collective-permute-start(bf16[512,1024]{1,0:T(8,128)(2,1)S(1)} %copy-done.226), channel_id=1, source_target_pairs={{0,4},{4,0},{8,12},{12,8},{16,20},{20,16},{24,28},{28,24},{1,5},{5... | collective-permute-start | bytes 3145736 | tf_op jit(solution)/shard_map/ppermute | solution.py:18
  698.7 20.8 %collective-permute-start.115 = (bf16[512,1024]{1,0:T(8,128)(2,1)S(1)}, bf16[512,1024]{1,0:T(8,128)(2,1)S(1)}, u32[]{:S(2)}, u32[]{:S(2)}) collective-permute-start(bf16[512,1024]{1,0:T(8,128)(2,1)S(1)} %copy-done.113), channel_id=1, source_target_pairs={{0,4},{4,0},{8,12},{12,8},{16,20},{20,16},{24,28},{28,24},{1,5},{5... | collective-permute-start | bytes 3145736 | tf_op jit(solution)/shard_map/ppermute | solution.py:18
  701.6 23.3 %collective-permute-start.121 = (bf16[2,128,1024]{2,1,0:T(8,128)(2,1)S(1)}, bf16[2,128,1024]{2,1,0:T(8,128)(2,1)S(1)}, u32[]{:S(2)}, u32[]{:S(2)}) collective-permute-start(bf16[2,128,1024]{2,1,0:T(8,128)(2,1)S(1)} %copy-done.162), channel_id=1, source_target_pairs={{0,16},{4,20},{8,24},{12,28},{16,0},{20,4},{24,8},{28,12},{1,17},{... | collective-permute-start | bytes 1572872 | tf_op jit(solution)/shard_map/ppermute | solution.py:18
  705.8 21.1 %collective-permute-start.105 = (bf16[2,128,1024]{2,1,0:T(8,128)(2,1)S(1)}, bf16[2,128,1024]{2,1,0:T(8,128)(2,1)S(1)}, u32[]{:S(2)}, u32[]{:S(2)}) collective-permute-start(bf16[2,128,1024]{2,1,0:T(8,128)(2,1)S(1)} %copy-done.161), channel_id=1, source_target_pairs={{0,8},{4,12},{8,0},{12,4},{16,24},{20,28},{24,16},{28,20},{1,9},{5... | collective-permute-start | bytes 1572872 | tf_op jit(solution)/shard_map/ppermute | solution.py:18
  708.4 20.5 %collective-permute-start.66 = (bf16[256,1024]{1,0:T(8,128)(2,1)S(1)}, bf16[256,1024]{1,0:T(8,128)(2,1)S(1)}, u32[]{:S(2)}, u32[]{:S(2)}) collective-permute-start(bf16[256,1024]{1,0:T(8,128)(2,1)S(1)} %copy-done.168), channel_id=1, source_target_pairs={{0,0},{1,1},{4,2},{5,3},{2,4},{3,5},{6,6},{7,7},{8,8},{9,9},{12,10... | collective-permute-start | bytes 1572872 | tf_op jit(solution)/shard_map/ppermute | solution.py:174
  714.4 24.3 %collective-permute-start.67 = (bf16[256,1024]{1,0:T(8,128)(2,1)S(1)}, bf16[256,1024]{1,0:T(8,128)(2,1)S(1)}, u32[]{:S(2)}, u32[]{:S(2)}) collective-permute-start(bf16[256,1024]{1,0:T(8,128)(2,1)S(1)} %copy-done.167), channel_id=1, source_target_pairs={{1,0},{0,1},{5,2},{4,3},{3,4},{2,5},{7,6},{6,7},{9,8},{8,9},{13,10... | collective-permute-start | bytes 1572872 | tf_op jit(solution)/shard_map/ppermute | solution.py:174
  719.5 24.9 %collective-permute-start.71 = (bf16[1,128,768]{2,1,0:T(8,128)(2,1)S(1)}, bf16[1,128,768]{2,1,0:T(8,128)(2,1)S(1)}, u32[]{:S(2)}, u32[]{:S(2)}) collective-permute-start(bf16[1,128,768]{2,1,0:T(8,128)(2,1)S(1)} %fusion.286), channel_id=1, source_target_pairs={{0,16},{4,20},{8,24},{12,28},{16,0},{20,4},{24,8},{28,12},{1,17},{... | collective-permute-start | bytes 589832 | tf_op jit(solution)/shard_map/ppermute | solution.py:18
  738.7 87.5 %collective-permute-start.122 = (bf16[1,128,1024]{2,1,0:T(8,128)(2,1)}, bf16[1,128,1024]{2,1,0:T(8,128)(2,1)}, u32[]{:S(2)}, u32[]{:S(2)}) collective-permute-start(bf16[1,128,1024]{2,1,0:T(8,128)(2,1)} %fusion.210), channel_id=1, source_target_pairs={{0,8},{4,12},{8,0},{12,4},{16,24},{20,28},{24,16},{28,20},{1,9},{5... | collective-permute-start | bytes 786440 | tf_op jit(solution)/shard_map/ppermute | solution.py:18
  741.6 22.3 %collective-permute-start.89 = (bf16[128,1024]{1,0:T(8,128)(2,1)S(1)}, bf16[128,1024]{1,0:T(8,128)(2,1)S(1)}, u32[]{:S(2)}, u32[]{:S(2)}) collective-permute-start(bf16[128,1024]{1,0:T(8,128)(2,1)S(1)} %pad_maximum_fusion.32), channel_id=1, source_target_pairs={{0,2},{1,3},{2,0},{3,1},{4,6},{5,7},{6,4},{7,5},{8,10},{9,11},{10,... | collective-permute-start | bytes 786440 | tf_op jit(solution)/shard_map/ppermute | solution.py:23
  741.8 22.8 %collective-permute-start.96 = (bf16[128,1024]{1,0:T(8,128)(2,1)S(1)}, bf16[128,1024]{1,0:T(8,128)(2,1)S(1)}, u32[]{:S(2)}, u32[]{:S(2)}) collective-permute-start(bf16[128,1024]{1,0:T(8,128)(2,1)S(1)} %pad_maximum_fusion.33), channel_id=1, source_target_pairs={{0,3},{1,0},{2,1},{3,2},{4,7},{5,4},{6,5},{7,6},{8,11},{9,8},{10,9... | collective-permute-start | bytes 786440 | tf_op jit(solution)/shard_map/ppermute | solution.py:23
  744.4 23.0 %collective-permute-start.124 = (bf16[2,128,1024]{2,1,0:T(8,128)(2,1)}, bf16[2,128,1024]{2,1,0:T(8,128)(2,1)}, u32[]{:S(2)}, u32[]{:S(2)}) collective-permute-start(bf16[2,128,1024]{2,1,0:T(8,128)(2,1)} %pad_maximum_fusion.22), channel_id=1, source_target_pairs={{0,16},{4,20},{8,24},{12,28},{16,0},{20,4},{24,8},{28,12},{1,17},{... | collective-permute-start | bytes 1572872 | tf_op jit(solution)/shard_map/ppermute | solution.py:18
  767.5 21.0 %collective-permute-start.112 = (bf16[2,128,1024]{2,1,0:T(8,128)(2,1)}, bf16[2,128,1024]{2,1,0:T(8,128)(2,1)S(1)}, u32[]{:S(2)}, u32[]{:S(2)}) collective-permute-start(bf16[2,128,1024]{2,1,0:T(8,128)(2,1)} %pad_maximum_fusion.19), channel_id=1, source_target_pairs={{0,8},{4,12},{8,0},{12,4},{16,24},{20,28},{24,16},{28,20},{1,9},{5... | collective-permute-start | bytes 1572872 | tf_op jit(solution)/shard_map/ppermute | solution.py:18
  770.4 29.2 %collective-permute-start.116 = (bf16[2,128,1024]{2,1,0:T(8,128)(2,1)}, bf16[2,128,1024]{2,1,0:T(8,128)(2,1)S(1)}, u32[]{:S(2)}, u32[]{:S(2)}) collective-permute-start(bf16[2,128,1024]{2,1,0:T(8,128)(2,1)} %pad_maximum_fusion.20), channel_id=1, source_target_pairs={{0,8},{4,12},{8,0},{12,4},{16,24},{20,28},{24,16},{28,20},{1,9},{5... | collective-permute-start | bytes 1572872 | tf_op jit(solution)/shard_map/ppermute | solution.py:18
  781.7 23.6 %collective-permute-start.125 = (bf16[1,128,1024]{2,1,0:T(8,128)(2,1)S(1)}, bf16[1,128,1024]{2,1,0:T(8,128)(2,1)S(1)}, u32[]{:S(2)}, u32[]{:S(2)}) collective-permute-start(bf16[1,128,1024]{2,1,0:T(8,128)(2,1)S(1)} %fusion.207), channel_id=1, source_target_pairs={{0,8},{4,12},{8,0},{12,4},{16,24},{20,28},{24,16},{28,20},{1,9},{5... | collective-permute-start | bytes 786440 | tf_op jit(solution)/shard_map/ppermute | solution.py:18
  783.9 27.0 %collective-permute-start.129 = (bf16[1,128,1024]{2,1,0:T(8,128)(2,1)S(1)}, bf16[1,128,1024]{2,1,0:T(8,128)(2,1)S(1)}, u32[]{:S(2)}, u32[]{:S(2)}) collective-permute-start(bf16[1,128,1024]{2,1,0:T(8,128)(2,1)S(1)} %fusion.204), channel_id=1, source_target_pairs={{0,8},{4,12},{8,0},{12,4},{16,24},{20,28},{24,16},{28,20},{1,9},{5... | collective-permute-start | bytes 786440 | tf_op jit(solution)/shard_map/ppermute | solution.py:18
  788.4 28.1 %collective-permute-start.133 = (bf16[1,128,1024]{2,1,0:T(8,128)(2,1)S(1)}, bf16[1,128,1024]{2,1,0:T(8,128)(2,1)S(1)}, u32[]{:S(2)}, u32[]{:S(2)}) collective-permute-start(bf16[1,128,1024]{2,1,0:T(8,128)(2,1)S(1)} %fusion.201), channel_id=1, source_target_pairs={{0,8},{4,12},{8,0},{12,4},{16,24},{20,28},{24,16},{28,20},{1,9},{5... | collective-permute-start | bytes 786440 | tf_op jit(solution)/shard_map/ppermute | solution.py:18
  817.6 20.6 %collective-permute-start.130 = (bf16[128,1024]{1,0:T(8,128)(2,1)S(1)}, bf16[128,1024]{1,0:T(8,128)(2,1)S(1)}, u32[]{:S(2)}, u32[]{:S(2)}) collective-permute-start(bf16[128,1024]{1,0:T(8,128)(2,1)S(1)} %fusion.203), channel_id=1, source_target_pairs={{0,2},{1,3},{2,0},{3,1},{4,6},{5,7},{6,4},{7,5},{8,10},{9,11},{10,... | collective-permute-start | bytes 786440 | tf_op jit(solution)/shard_map/ppermute | solution.py:23
  822.6 31.9 %collective-permute-start.134 = (bf16[128,1024]{1,0:T(8,128)(2,1)S(1)}, bf16[128,1024]{1,0:T(8,128)(2,1)S(1)}, u32[]{:S(2)}, u32[]{:S(2)}) collective-permute-start(bf16[128,1024]{1,0:T(8,128)(2,1)S(1)} %fusion.200), channel_id=1, source_target_pairs={{0,3},{1,0},{2,1},{3,2},{4,7},{5,4},{6,5},{7,6},{8,11},{9,8},{10,9... | collective-permute-start | bytes 786440 | tf_op jit(solution)/shard_map/ppermute | solution.py:23
  824.9 32.1 %collective-permute-start.106 = (bf16[1,128,1024]{2,1,0:T(8,128)(2,1)S(1)}, bf16[1,128,1024]{2,1,0:T(8,128)(2,1)}, u32[]{:S(2)}, u32[]{:S(2)}) collective-permute-start(bf16[1,128,1024]{2,1,0:T(8,128)(2,1)S(1)} %fusion.222), channel_id=1, source_target_pairs={{0,16},{4,20},{8,24},{12,28},{16,0},{20,4},{24,8},{28,12},{1,17},{... | collective-permute-start | bytes 786440 | tf_op jit(solution)/shard_map/ppermute | solution.py:18
  826.2 30.7 %collective-permute-start.110 = (bf16[128,1024]{1,0:T(8,128)(2,1)}, bf16[128,1024]{1,0:T(8,128)(2,1)}, u32[]{:S(2)}, u32[]{:S(2)}) collective-permute-start(bf16[128,1024]{1,0:T(8,128)(2,1)} %fusion.218), channel_id=1, source_target_pairs={{0,1},{1,2},{2,3},{3,0},{4,5},{5,6},{6,7},{7,4},{8,9},{9,10},{10,1... | collective-permute-start | bytes 786440 | tf_op jit(solution)/shard_map/ppermute | solution.py:23
  826.2 34.6 %collective-permute-start.114 = (bf16[128,1024]{1,0:T(8,128)(2,1)}, bf16[128,1024]{1,0:T(8,128)(2,1)}, u32[]{:S(2)}, u32[]{:S(2)}) collective-permute-start(bf16[128,1024]{1,0:T(8,128)(2,1)} %fusion.215), channel_id=1, source_target_pairs={{0,2},{1,3},{2,0},{3,1},{4,6},{5,7},{6,4},{7,5},{8,10},{9,11},{10,... | collective-permute-start | bytes 786440 | tf_op jit(solution)/shard_map/ppermute | solution.py:23
  838.3 27.6 %collective-permute-start.118 = (bf16[128,1024]{1,0:T(8,128)(2,1)}, bf16[128,1024]{1,0:T(8,128)(2,1)}, u32[]{:S(2)}, u32[]{:S(2)}) collective-permute-start(bf16[128,1024]{1,0:T(8,128)(2,1)} %fusion.212), channel_id=1, source_target_pairs={{0,3},{1,0},{2,1},{3,2},{4,7},{5,4},{6,5},{7,6},{8,11},{9,8},{10,9... | collective-permute-start | bytes 786440 | tf_op jit(solution)/shard_map/ppermute | solution.py:23
  (311 other events, 3001.7 us)

commit v2 on v1

--- a/solution.py
+++ b/solution.py
@@ -1,12 +1,17 @@
 import jax
 import jax.numpy as jnp
 from jax import lax
+from jax.experimental import pallas as pl
+from jax.experimental.pallas import tpu as pltpu
 from jax.sharding import PartitionSpec as P
 
 HD = 64
 EPS = 1e-05
 BF = jnp.bfloat16
 F32 = jnp.float32
+MESH = pl.DeviceIdType.MESH
+T = 512
+PART = 128
 
 
 def dot(a, b, ca, cb):
@@ -126,7 +131,7 @@
     )
 
 
-def body(
+def plain_body(
     cells,
     lengths,
     query_matrix,
@@ -321,6 +326,801 @@
         jnp.sum(e2 * unit_two, 0),
         jnp.sum(e2, 0),
         jnp.sum(g, 0),
+    ]
+    split_dp = [jnp.roll(jnp.swapaxes(s.reshape(n_dp, n_mp, -1), 0, 1), -z, 0) for s in sums]
+    packed = jnp.concatenate(split_mp + split_dp, 2)
+    packed = jnp.take(packed, jnp.arange(n_dp) ^ d, axis=1)
+    packed = packed[:, 0::2] + cross(packed[:, 1::2], 0)
+    packed = scatter({2 * i: packed[:, i] for i in range(packed.shape[1])}, False)
+    vec = packed[0]
+    for r in range(1, n_mp):
+        vec = vec + shift(packed[r], r)
+    nq = split_mp[0].shape[2]
+    nu = split_mp[2].shape[2]
+    ns = split_dp[0].shape[2]
+    vq, vv, vu = vec[:nq], vec[nq : 2 * nq], vec[2 * nq : 2 * nq + nu]
+    rest = [vec[2 * nq + nu + i * ns : 2 * nq + nu + (i + 1) * ns] for i in range(6)]
+    return (
+        out_cells,
+        grad_cells,
+        grad_attn[:, :hw],
+        grad_attn[:, hw : 2 * hw],
+        grad_attn[:, 2 * hw : 3 * hw],
+        vq,
+        vv,
+        grad_attn[:, 3 * hw :].T,
+        rest[0],
+        rest[1],
+        rest[2],
+        rest[3],
+        rest[4],
+        grad_up,
+        vu,
+        grad_down,
+        rest[5],
+    )
+
+
+def dg(a, b, ca, cb):
+    return lax.dot_general(a, b, (((ca,), (cb,)), ((), ())), preferred_element_type=F32)
+
+
+def lane_block(start, size=128):
+    return pl.ds(pl.multiple_of(start, size), size)
+
+
+class Place:
+    def __init__(self):
+        self.d, self.z = lax.axis_index("dp"), lax.axis_index("mp")
+        self.bit = [lax.rem(self.d // (1 << b), 2) for b in range(3)]
+        self.core = self.bit[0]
+        self.base = self.d - self.core
+
+    def across(self, i):
+        v = self.d
+        for b in range(3):
+            if i >> b & 1:
+                v = v + (1 << b) * (1 - 2 * self.bit[b])
+        return v
+
+    def rows(self, i):
+        return lane_block(self.across(i) * PART, PART)
+
+    def greet(self):
+        barrier = pltpu.get_barrier_semaphore()
+        for step in range(1, 4):
+            for c in range(2):
+                pl.semaphore_signal(
+                    barrier,
+                    inc=1,
+                    device_id=(self.base + c, lax.rem(self.z + step, 4)),
+                    device_id_type=MESH,
+                )
+        for i in (1, 2, 4):
+            pl.semaphore_signal(barrier, inc=1, device_id=(self.across(i), self.z), device_id_type=MESH)
+        pl.semaphore_wait(barrier, 9)
+
+
+def remote(src, dst, send, recv, device):
+    return pltpu.make_async_remote_copy(
+        src_ref=src, dst_ref=dst, send_sem=send, recv_sem=recv, device_id=device, device_id_type=MESH
+    )
+
+
+class Unit:
+    def __init__(self, place, own, at, parts, zsend, zrecv, send, recv, flip):
+        self.p, self.own, self.at, self.parts = place, own, at, parts
+        self.zsend, self.zrecv, self.send, self.recv = zsend, zrecv, send, recv
+        self.first, self.second = (4, 2) if flip else (2, 4)
+
+    def along(self, k, slot_from, slot_to, right):
+        p = self.p
+        device = (p.d, p.z + 1 if right else p.z - 1)
+        return [
+            remote(
+                self.own(q) if slot_from is None else self.at(slot_from, 0, q),
+                self.at(slot_to, 0, q),
+                self.zsend.at[k, q],
+                self.zrecv.at[slot_to - 1, q],
+                device,
+            )
+            for q in range(self.parts)
+        ]
+
+    def steps(self):
+        z = self.p.z
+        inner = jnp.logical_and(z >= 1, z <= 2)
+        return [
+            (z <= 2, (0, None, 3, True)),
+            (z >= 1, (1, None, 1, False)),
+            (inner, (2, 3, 2, True)),
+            (inner, (3, 1, 2, False)),
+            (z == 1, (4, 2, 3, False)),
+            (z == 2, (5, 2, 1, True)),
+        ]
+
+    def go(self, k):
+        cond, what = self.steps()[k]
+
+        @pl.when(cond)
+        def _():
+            for c in self.along(*what):
+                c.start()
+
+    def start(self):
+        self.go(0)
+        self.go(1)
+
+    def landed(self, slot):
+        for q in range(self.parts):
+            here = self.at(slot, 0, q)
+            remote(here, here, self.zsend.at[0, q], self.zrecv.at[slot - 1, q], (self.p.across(1), self.p.z)).wait_recv()
+
+    def xy(self, slot, k, i, bit):
+        here = self.at(slot, i, None)
+        return remote(
+            here,
+            here,
+            self.send.at[slot - 1, k],
+            self.recv.at[slot - 1, i ^ bit],
+            (self.p.across(bit), self.p.z),
+        )
+
+    def arrived(self, slot, i):
+        here = self.at(slot, i, None)
+        remote(here, here, self.send.at[slot - 1, 0], self.recv.at[slot - 1, i], (self.p.across(1), self.p.z)).wait_recv()
+
+    def one(self, slot):
+        self.xy(slot, 0, 0, self.first).start()
+
+    def z_one(self):
+        z = self.p.z
+
+        @pl.when(z >= 1)
+        def _():
+            self.landed(3)
+
+        self.go(2)
+
+        @pl.when(z <= 2)
+        def _():
+            self.landed(1)
+
+        self.go(3)
+
+        @pl.when(z >= 1)
+        def _():
+            self.one(3)
+
+        @pl.when(z <= 2)
+        def _():
+            self.one(1)
+
+    def z_two(self):
+        self.landed(2)
+        self.go(4)
+        self.go(5)
+        self.one(2)
+
+    def z_three(self):
+        z = self.p.z
+
+        @pl.when(z == 0)
+        def _():
+            self.landed(3)
+            self.one(3)
+
+        @pl.when(z == 3)
+        def _():
+            self.landed(1)
+            self.one(1)
+
+    def two(self, slot):
+        self.arrived(slot, self.first)
+        self.xy(slot, 1, 0, self.second).start()
+        self.xy(slot, 2, self.first, self.second).start()
+
+    def three(self, slot):
+        self.arrived(slot, self.second)
+        self.arrived(slot, self.first + self.second)
+        for k, i in enumerate((0, 2, 4, 6)):
+            self.xy(slot, 3 + k, i, 1).start()
+
+    def whole(self, slot):
+        for i in (1, 3, 5, 7):
+            self.arrived(slot, i)
+
+    def finish(self):
+        for k in range(6):
+            cond, what = self.steps()[k]
+
+            @pl.when(cond)
+            def _(what=what):
+                for c in self.along(*what):
+                    c.wait_send()
+
+        for slot in (1, 2, 3):
+            self.xy(slot, 0, 0, self.first).wait_send()
+            self.xy(slot, 1, 0, self.second).wait_send()
+            self.xy(slot, 2, self.first, self.second).wait_send()
+            for k, i in enumerate((0, 2, 4, 6)):
+                self.xy(slot, 3 + k, i, 1).wait_send()
+
+
+def bring_copies(p, src, dst, sends, recvs, here):
+    for s in range(2):
+        target = (p.base + p.z // 2, 2 * p.core + s)
+        half = lax.rem(p.z, 2)
+        rows = lane_block(half * 256, 256)
+        same = jnp.logical_and(p.core == p.z // 2, p.z == 2 * p.core + s)
+
+        @pl.when(same)
+        def _():
+            pltpu.make_async_copy(src.at[s], dst.at[rows], here).start()
+
+        @pl.when(jnp.logical_not(same))
+        def _():
+            remote(src.at[s], dst.at[rows], sends.at[s], recvs.at[half], target).start()
+
+
+def bring_wait(p, dst, recvs, here):
+    for half in range(2):
+        block = dst.at[pl.ds(half * 256, 256)]
+        same = jnp.logical_and(p.core == p.z // 2, lax.rem(p.z, 2) == half)
+
+        @pl.when(same)
+        def _():
+            pltpu.make_async_copy(block, block, here).wait()
+
+        @pl.when(jnp.logical_not(same))
+        def _():
+            remote(block, block, recvs.at[half], recvs.at[half], (p.across(1), p.z)).wait_recv()
+
+
+def bring_sent(p, src, sends):
+    for s in range(2):
+        same = jnp.logical_and(p.core == p.z // 2, p.z == 2 * p.core + s)
+
+        @pl.when(jnp.logical_not(same))
+        def _():
+            remote(src.at[s], src.at[s], sends.at[s], sends.at[s], (p.across(1), p.z)).wait_send()
+
+
+def norm_stats(x):
+    center = x - jnp.mean(x, -1, keepdims=True)
+    inverse = lax.rsqrt(jnp.mean(center * center, -1, keepdims=True) + EPS)
+    return center * inverse, inverse
+
+
+def each_rows(size, total, f):
+    def step(i, carry):
+        f(pl.ds(pl.multiple_of(i * size, size), size))
+        return carry
+
+    lax.fori_loop(0, total // size, step, 0)
+
+
+def chosen_both(p, t_ref, both_ref, sends, recvs):
+    copies = []
+    for k, i in enumerate((0, 2, 4, 6)):
+        block = pl.ds(k * PART, PART)
+        both_ref[block, 0:T] = t_ref[p.rows(i), :]
+        copies.append(
+            remote(
+                t_ref.at[p.rows(i ^ 1)],
+                both_ref.at[block, T : 2 * T],
+                sends.at[k],
+                recvs.at[k],
+                (p.across(1), p.z),
+            )
+        )
+    for c in copies:
+        c.start()
+    return copies
+
+
+def forward_kernel(
+    cells, grad, len_own, wq, wk, wv, wo, up, down, small_own, b_out, gain1, shift1, gain2, shift2, b_down,
+    x_out, rows1_out, q_out, k_out, v_out, mix_out, e_out, r_out, wa_out, wo_out, wu, wd, res_out, dm_out, gu_out, gd_out, vec_out,
+    xv, gv, rows1, wav, wov, qv, kv, vv, mix, eb, rv, bias, vt, ot, middle, rows2, tt, xb, gb, acc, e2,
+    uv, dv, ho, du, hs, ds, gus, gds, len_sib, small1, small2, small3,
+    a_zs, a_zr, a_s, a_r, o_zs, o_zr, o_s, o_r, u_zs, u_zr, u_s, u_r, d_zs, d_zr, d_s, d_r,
+    act_s, act_r, sm_s, sm_r, kv_s, kv_r, both_s, both_r, hd_s, hd_r, credit, loc, load, store,
+):
+    p = Place()
+    small = [small_own, small1, small2, small3]
+    sibling = (p.across(1), p.z)
+
+    ws = (wq, wk, wv)
+    own_rows = p.rows(0)
+
+    def a_at(slot, i, part):
+        if part is None:
+            return wav.at[slot, p.rows(i)]
+        return wav.at[slot, p.rows(i), pl.ds(part * 256, 256)]
+
+    unit_a = Unit(p, lambda q: ws[q].at[own_rows], a_at, 3, a_zs, a_zr, a_s, a_r, False)
+    unit_o = Unit(
+        p,
+        lambda q: wo.at[:, own_rows],
+        lambda slot, i, q: wov.at[pl.ds(slot * 256, 256), p.rows(i)],
+        1, o_zs, o_zr, o_s, o_r, True,
+    )
+    unit_u = Unit(p, lambda q: up.at[own_rows], lambda slot, i, q: wu.at[slot - 1, p.rows(i)], 1, u_zs, u_zr, u_s, u_r, False)
+    unit_d = Unit(p, lambda q: down.at[own_rows], lambda slot, i, q: wd.at[slot - 1, p.rows(i)], 1, d_zs, d_zr, d_s, d_r, True)
+
+    own_loads = [pltpu.make_async_copy(w, wav.at[0, :, pl.ds(k * 256, 256)], loc.at[k]) for k, w in enumerate(ws)]
+    own_loads.append(pltpu.make_async_copy(wo, wov.at[pl.ds(0, 256)], loc.at[3]))
+    for c in own_loads:
+        c.start()
+    first_loads = [pltpu.make_async_copy(up, uv.at[0], load.at[0, 0]), pltpu.make_async_copy(down, dv.at[0], load.at[1, 0])]
+    for c in first_loads:
+        c.start()
+
+    p.greet()
+    unit_a.start()
+    bring_copies(p, cells, xv, act_s.at[0], act_r.at[0], loc.at[4])
+    small_copies = []
+    for r in (1, 2, 3):
+        small_copies.append(remote(small_own, small[r], sm_s.at[r], sm_r.at[r], (p.d, lax.rem(p.z + 4 - r, 4))))
+    small_copies.append(remote(len_own, len_sib, sm_s.at[0], sm_r.at[0], sibling))
+    for c in small_copies:
+        c.start()
+    unit_a.z_one()
+    unit_a.z_two()
+    unit_a.z_three()
+    unit_o.start()
+    unit_u.start()
+    for slot in (1, 3, 2):
+        unit_a.two(slot)
+
+    bring_wait(p, xv, act_r.at[0], loc.at[4])
+    bring_copies(p, grad, gv, act_s.at[1], act_r.at[1], loc.at[5])
+    unit_d.start()
+
+    def first_norm(rows):
+        unit, _ = norm_stats(xv[rows, :].astype(F32))
+        rows1[rows, :] = (unit * gain1[...] + shift1[...]).astype(BF)
+
+    each_rows(128, T, first_norm)
+    outs = [pltpu.make_async_copy(xv, x_out, store.at[0]), pltpu.make_async_copy(rows1, rows1_out, store.at[1])]
+    for c in outs:
+        c.start()
+    for slot in (1, 3, 2):
+        unit_a.three(slot)
+    unit_o.z_one()
+    unit_o.z_two()
+    unit_o.z_three()
+    unit_u.z_one()
+
+    small_copies[3].wait_recv()
+    slot_row = lax.rem(p.z, 2)
+    near = jnp.where(p.z // 2 == p.core, 1.0, 0.0)
+    length = near * len_own[pl.ds(slot_row, 1), :] + (1.0 - near) * len_sib[pl.ds(slot_row, 1), :]
+    length = length[:, :1]
+    lane = lax.broadcasted_iota(jnp.int32, (1, 128), 1)
+    key = lax.broadcasted_iota(jnp.int32, (2 * T, 128), 0)
+    key = jnp.where(key < T, key + p.core * T, key - T + (1 - p.core) * T)
+    barred = jnp.where(key.astype(F32) < length, 0.0, -1e30)
+    bias[0] = jnp.where(lane == 64, barred, 0.0).astype(BF)
+    bias[1] = jnp.where(lane == 0, barred, 0.0).astype(BF)
+
+    def kept(rows_start, size):
+        row = lax.broadcasted_iota(jnp.int32, (size, 1), 0) + rows_start + p.core * T
+        return row.astype(F32) < length
+
+    for c in own_loads:
+        c.wait()
+    for r in (1, 2, 3):
+        small_copies[r - 1].wait_recv()
+
+    kv_copies = []
+
+    def project(r):
+        b = small[r]
+        x = rows1[...]
+        qv[r] = (dg(x, wav[r, :, 0:256], 1, 0) + b[:, 0:256]).astype(BF)
+        kv[r, 0:T, :] = dg(x, wav[r, :, 256:512], 1, 0).astype(BF)
+        vv[r, 0:T, :] = (dg(x, wav[r, :, 512:768], 1, 0) + b[:, 256:512]).astype(BF)
+        cs = [
+            remote(ref.at[r, pl.ds(0, T)], ref.at[r, pl.ds(T, T)], kv_s.at[r, n], kv_r.at[r, n], sibling)
+            for n, ref in enumerate((kv, vv))
+        ]
+        for c in cs:
+            c.start()
+        kv_copies.append(cs)
+
+    def e_copy(head, slot):
+        return pltpu.make_async_copy(eb.at[slot], e_out.at[head], store.at[2 + slot])
+
+    def attend(r):
+        for c in kv_copies[r]:
+            c.wait_recv()
+        vt[...] = jnp.transpose(vv[r], (1, 0))
+
+        def pair(j, carry):
+            cols = lane_block(j * 128)
+            kp = kv[r, :, cols]
+            qp = qv[r, :, cols] * BF(HD**-0.5)
+            for h in range(2):
+                mine = (lane < 64) if h == 0 else (lane >= 64)
+                one = lane == (64 if h == 0 else 0)
+                ka = jnp.where(mine, kp, bias[h])
+                qa = jnp.where(mine, qp, jnp.where(one, BF(1), BF(0)))
+                s = dg(ka, qa, 1, 1)
+                e = jnp.exp(s - jnp.max(s, 0, keepdims=True))
+                inv = 1.0 / jnp.sum(e, 0, keepdims=True)
+                head = r * 4 + 2 * j + h
+                if r == 0:
+                    @pl.when(j > 0)
+                    def _():
+                        e_copy(head - 2, h).wait()
+                else:
+                    e_copy(head - 2, h).wait()
+                eb[h] = e.astype(BF)
+                e_copy(head, h).start()
+                feats = pl.ds(pl.multiple_of(j * 128 + h * 64, 64), 64)
+                ot[feats, :] = (dg(vt[feats, :], eb[h], 1, 0) * inv).astype(BF)
+                rv[head] = inv
+            return carry
+
+        lax.fori_loop(0, 2, pair, 0)
+        mix[:, r * 256 : (r + 1) * 256] = jnp.transpose(ot[...], (1, 0))
+
+    project(0)
+    unit_u.z_two()
+    for slot in (1, 2, 3):
+        unit_a.whole(slot)
+    project(1)
+    unit_u.z_three()
+    for slot in (1, 3, 2):
+        unit_o.two(slot)
+    attend(0)
+    unit_d.z_one()
+    project(2)
+    project(3)
+    for slot in (1, 3, 2):
+        unit_o.three(slot)
+        unit_u.two(slot)
+    unit_d.z_two()
+    unit_d.z_three()
+    attend(1)
+    for slot in (1, 3, 2):
+        unit_u.three(slot)
+        unit_d.two(slot)
+    attend(2)
+    for slot in (1, 3, 2):
+        unit_d.three(slot)
+        unit_o.whole(slot)
+    attend(3)
+    for h in range(2):
+        e_copy(14 + h, h).wait()
+
+    outs += [
+        pltpu.make_async_copy(wav, wa_out, store.at[4]),
+        pltpu.make_async_copy(wov, wo_out, store.at[5]),
+        pltpu.make_async_copy(qv, q_out, store.at[6]),
+        pltpu.make_async_copy(kv, k_out, store.at[7]),
+        pltpu.make_async_copy(vv, v_out, store.at[8]),
+        pltpu.make_async_copy(mix, mix_out, store.at[9]),
+        pltpu.make_async_copy(rv, r_out, store.at[10]),
+    ]
+    for c in outs[2:]:
+        c.start()
+
+    for n in range(2):
+        cols = pl.ds(n * 512, 512)
+        middle[:, cols] = dg(mix[...], wov[:, cols], 1, 0)
+
+    def second_norm(rows):
+        m = middle[rows, :] + xv[rows, :].astype(F32) + b_out[...]
+        middle[rows, :] = m
+        unit, _ = norm_stats(m)
+        rows2[rows, :] = (unit * gain2[...] + shift2[...]).astype(BF)
+        acc[rows, :] = m + b_down[...]
+
+    each_rows(128, T, second_norm)
+    tt[...] = jnp.transpose(rows2[...], (1, 0))
+    both = chosen_both(p, tt, xb, both_s.at[0], both_r.at[0])
+    bring_wait(p, gv, act_r.at[1], loc.at[5])
+
+    def mask_grad(i, carry):
+        rows = pl.ds(pl.multiple_of(i * 128, 128), 128)
+        gv[rows, :] = jnp.where(kept(i * 128, 128), gv[rows, :].astype(F32), 0.0).astype(BF)
+        return carry
+
+    lax.fori_loop(0, T // 128, mask_grad, 0)
+    for c in both:
+        c.wait_send()
+    tt[...] = jnp.transpose(gv[...], (1, 0))
+    both2 = chosen_both(p, tt, gb, both_s.at[1], both_r.at[1])
+
+    order = (0, 1, 3, 2)
+
+    def load_copies(n):
+        r = order[n]
+        return [
+            pltpu.make_async_copy(wu.at[r - 1], uv.at[n % 2], load.at[0, n % 2]),
+            pltpu.make_async_copy(wd.at[r - 1], dv.at[n % 2], load.at[1, n % 2]),
+        ]
+
+    def hidden(n):
+        r, slot = order[n], n % 2
+        for k in range(2):
+            c = pl.ds(k * 512, 512)
+            upper = dg(rows2[...], uv[slot, :, c], 1, 0) + small[r][:, 512 + k * 512 : 1024 + k * 512]
+            act, slope = gelu_pair(upper)
+            ho[slot, :, c] = act.astype(BF)
+            d_up = (dg(gv[...], dv[slot, c, :], 1, 1) * slope).astype(BF)
+            du[slot, :, c] = d_up
+            vec_out[r : r + 1, c] = jnp.sum(d_up.astype(F32), 0, keepdims=True)
+        if n >= 2:
+            pl.semaphore_wait(credit, 1)
+        cs = [
+            remote(ho.at[slot], hs.at[slot], hd_s.at[0, slot], hd_r.at[0, slot], sibling),
+            remote(du.at[slot], ds.at[slot], hd_s.at[1, slot], hd_r.at[1, slot], sibling),
+        ]
+        for c in cs:
+            c.start()
+        for k in range(2):
+            c = pl.ds(k * 512, 512)
+            acc[:, c] = acc[:, c] + dg(ho[slot], dv[slot, :, c], 1, 0)
+            new = dg(du[slot], uv[slot, c, :], 1, 1)
+            e2[:, c] = new if n == 0 else e2[:, c] + new
+        return cs
+
+    g_stores = [None, None]
+
+    def weight_grads(n, cs):
+        r, slot = order[n], n % 2
+        for c in cs:
+            c.wait_recv()
+        if n >= 1:
+            for c in g_stores:
+                c.wait()
+        gus[...] = (dg(xb[:, 0:T], du[slot], 1, 0) + dg(xb[:, T : 2 * T], ds[slot], 1, 0)).astype(BF)
+        gds[...] = (dg(gb[:, 0:T], ho[slot], 1, 0) + dg(gb[:, T : 2 * T], hs[slot], 1, 0)).astype(BF)
+        if n < 2:
+            pl.semaphore_signal(credit, inc=1, device_id=sibling, device_id_type=MESH)
+        g_stores[0] = pltpu.make_async_copy(gus, gu_out.at[r], store.at[11])
+        g_stores[1] = pltpu.make_async_copy(gds, gd_out.at[r], store.at[12])
+        for c in g_stores:
+            c.start()
+        for c in cs:
+            c.wait_send()
+
+    for c in first_loads:
+        c.wait()
+    held = [hidden(0)]
+    for n in range(1, 4):
+        unit_u.whole(order[n])
+        unit_d.whole(order[n])
+        cs = load_copies(n)
+        for c in cs:
+            c.start()
+        if n == 1:
+            for c in both + both2:
+                c.wait_recv()
+        if n >= 2:
+            weight_grads(n - 2, held[n - 2])
+        for c in cs:
+            c.wait()
+        held.append(hidden(n))
+    weight_grads(2, held[2])
+    weight_grads(3, held[3])
+
+    vec_out[4:16, :] = jnp.zeros((12, width_of(vec_out)), F32)
+
+    def last(i, carry):
+        rows = pl.ds(pl.multiple_of(i * 128, 128), 128)
+        res = jnp.where(kept(i * 128, 128), acc[rows, :], 0.0)
+        rows2[rows, :] = res.astype(BF)
+        unit, inverse = norm_stats(middle[rows, :])
+        e = e2[rows, :]
+        g = gv[rows, :].astype(F32)
+        u = e * gain2[...]
+        d_mid = g + inverse * (u - jnp.mean(u, -1, keepdims=True) - unit * jnp.mean(u * unit, -1, keepdims=True))
+        middle[rows, :] = d_mid
+        for k, v in enumerate((d_mid, e * unit, e, g)):
+            vec_out[4 + k : 5 + k, :] += jnp.sum(v, 0, keepdims=True)
+        return carry
+
+    lax.fori_loop(0, T // 128, last, 0)
+    ends = [pltpu.make_async_copy(rows2, res_out, store.at[13]), pltpu.make_async_copy(middle, dm_out, store.at[14])]
+    for c in ends:
+        c.start()
+    for c in ends + outs + g_stores:
+        c.wait()
+    for c in both2 + small_copies:
+        c.wait_send()
+    for cs in kv_copies:
+        for c in cs:
+            c.wait_send()
+    for unit in (unit_a, unit_o, unit_u, unit_d):
+        unit.finish()
+    bring_sent(p, cells, act_s.at[0])
+    bring_sent(p, grad, act_s.at[1])
+
+
+def width_of(ref):
+    return ref.shape[-1]
+
+def forward(*args):
+    s = jax.ShapeDtypeStruct
+    outs = [
+        (T, 1024), (T, 1024), (4, T, 256), (4, 2 * T, 256), (4, 2 * T, 256), (T, 1024), (16, 2 * T, T), (16, 1, T),
+        (4, 1024, 768), (1024, 1024), (3, 1024, 1024), (3, 1024, 1024), (T, 1024), (T, 1024), (4, T, 1024), (4, T, 1024), (16, 1024),
+    ]
+    wide = (7, 13, 16)
+    hbm, fast = pl.BlockSpec(memory_space=pltpu.HBM), pl.BlockSpec(memory_space=pltpu.VMEM)
+    b, f, dma = (lambda *x: pltpu.VMEM(x, BF)), (lambda *x: pltpu.VMEM(x, F32)), (lambda *x: pltpu.SemaphoreType.DMA(x))
+    sems = []
+    for parts in (3, 1, 1, 1):
+        sems += [dma(6, parts), dma(3, parts), dma(3, 7), dma(3, 8)]
+    return pl.pallas_call(
+        forward_kernel,
+        out_shape=[s(o, F32 if n in wide else BF) for n, o in enumerate(outs)],
+        in_specs=[hbm, hbm, fast] + [hbm] * 6 + [fast] * 7,
+        out_specs=[hbm] * 16 + [fast],
+        scratch_shapes=[
+            b(T, 1024), b(T, 1024), b(T, 1024), b(4, 1024, 768), b(1024, 1024), b(4, T, 256), b(4, 2 * T, 256), b(4, 2 * T, 256),
+            b(T, 1024), b(2, 2 * T, T), f(16, 1, T), b(2, 2 * T, 128), b(256, 2 * T), b(256, T), f(T, 1024), b(T, 1024),
+            b(1024, T), b(T, 2 * T), b(T, 2 * T), f(T, 1024), f(T, 1024),
+            b(2, 1024, 1024), b(2, 1024, 1024), b(2, T, 1024), b(2, T, 1024), b(2, T, 1024), b(2, T, 1024), b(T, 1024), b(T, 1024),
+            f(8, 128), f(1, 1536), f(1, 1536), f(1, 1536),
+        ]
+        + sems
+        + [dma(2, 2), dma(2, 2), dma(4), dma(4), dma(4, 2), dma(4, 2), dma(2, 4), dma(2, 4), dma(2, 2), dma(2, 2),
+           pltpu.SemaphoreType.REGULAR, dma(6), dma(2, 2), dma(15)],
+        compiler_params=pltpu.CompilerParams(collective_id=0, has_side_effects=True, vmem_limit_bytes=62 * 2**20),
+    )(*args)
+
+
+def body(*args):
+    if lax.axis_size("dp") == 8 and lax.axis_size("mp") == 4:
+        return fused_body(*args)
+    return plain_body(*args)
+
+
+def fused_body(
+    cells,
+    lengths,
+    query_matrix,
+    key_matrix,
+    value_matrix,
+    query_bias,
+    value_bias,
+    output_matrix,
+    b_out,
+    gain_one,
+    shift_one,
+    gain_two,
+    shift_two,
+    expand_weight,
+    expand_bias,
+    contract_weight,
+    b_down,
+    grad_out,
+):
+    slots, rows, width = cells.shape
+    n_dp, n_mp = lax.axis_size("dp"), lax.axis_size("mp")
+    d, z = lax.axis_index("dp"), lax.axis_index("mp")
+    per = n_mp // slots
+    core = d % per
+    tokens = slots * rows
+    part = width // n_dp
+    hw = query_matrix.shape[1]
+    turns = moves(n_dp, n_mp, slots)
+
+    def bring(x):
+        got = [
+            lax.ppermute(
+                lax.dynamic_index_in_dim(x, (t + z) % slots, 0, False), ("dp", "mp"), turns[t]
+            )
+            for t in range(slots)
+        ]
+        even = z % slots == 0
+        return jnp.concatenate(
+            [jnp.where(even, got[0], got[1]), jnp.where(even, got[1], got[0])], 0
+        )
+
+    def give_back(x):
+        x = x.reshape(slots, rows, width)
+        got = [
+            lax.ppermute(
+                lax.dynamic_index_in_dim(x, (t + z) % slots, 0, False),
+                ("dp", "mp"),
+                [(b, a) for a, b in turns[t]],
+            )
+            for t in range(slots)
+        ]
+        even = z % slots == 0
+        return jnp.stack(
+            [jnp.where(even, got[0], got[1]), jnp.where(even, got[1], got[0])], 0
+        )
+
+    row = lambda v: v.reshape(1, -1)
+    small = row(jnp.concatenate([query_bias, value_bias, expand_bias]))
+    len_own = jnp.pad(jnp.broadcast_to(lengths.astype(F32)[:, None], (slots, 128)), ((0, 8 - slots), (0, 0)))
+    (x, rows_one, q_all, k_all, v_all, mixed_all, e_all, r_all, wa, wo, _, _, res, d_middle, gu, gd, vec) = forward(
+        cells, grad_out, len_own, query_matrix, key_matrix, value_matrix, output_matrix, expand_weight, contract_weight,
+        small, row(b_out), row(gain_one), row(shift_one), row(gain_two), row(shift_two), row(b_down),
+    )
+    _, unit_one, inv_one = layer_norm(x.astype(F32), gain_one, shift_one)
+
+    order = jnp.arange(0, n_dp, 2) ^ d
+
+    def chosen(v):
+        return jnp.take(v.reshape(v.shape[0], n_dp, part), order, axis=1).reshape(v.shape[0], -1)
+
+    def other(v):
+        return jnp.take(v.reshape(v.shape[0], n_dp, part), order ^ 1, axis=1).reshape(v.shape[0], -1)
+
+    def both_cores(v):
+        return jnp.concatenate([chosen(v), cross(other(v), 0)], 0)
+
+    def weight_grad(left, right, flip):
+        right = jnp.concatenate([right, cross(right, 0)], 0)
+        return weight_grad_all(left, right, flip)
+
+    def weight_grad_all(left, right, flip):
+        got = dot(left, right, 0, 0).astype(BF).reshape(-1, part, right.shape[1])
+        return scatter({2 * i: got[i] for i in range(got.shape[0])}, flip)
+
+    def finish(pieces):
+        total = pieces[0].astype(F32)
+        for r in range(1, n_mp):
+            total = total + shift(pieces[r], r).astype(F32)
+        return total
+
+    def plane(block, flip):
+        got = block.reshape(-1, part, block.shape[-1])
+        return scatter({2 * i: got[i] for i in range(got.shape[0])}, flip)
+
+    up_parts = [plane(gu[r], False) for r in range(n_mp)]
+    down_parts = [plane(gd[r], True) for r in range(n_mp)]
+    b_up = [vec[r] for r in range(n_mp)]
+    out_cells = give_back(res)
+    grad_up = finish(up_parts)
+    grad_down = finish(down_parts).T
+    gm = d_middle.astype(BF)
+    gm_both = both_cores(gm)
+    one_both = both_cores(rows_one)
+    e1 = jnp.zeros((tokens, width), F32)
+    a_parts, b_q, b_v = [], [], []
+    for r in range(n_mp):
+        q, k, v, mixed = q_all[r], k_all[r], v_all[r], mixed_all[:, r * hw : (r + 1) * hw]
+        heads = hw // HD
+        p = jnp.swapaxes(e_all[r * heads : (r + 1) * heads].astype(F32) * r_all[r * heads : (r + 1) * heads], 1, 2).astype(BF)
+        w = wa[r]
+        d_mixed = dot(gm, wo[r * hw : (r + 1) * hw], 1, 1).astype(BF)
+        dq, dk, dv = attend_back(q, k, v, p, mixed, d_mixed)
+        dk_all = (dk.astype(F32) + jnp.roll(cross(dk, 0), tokens, 0).astype(F32)).astype(BF)
+        dv_all = (dv.astype(F32) + jnp.roll(cross(dv, 0), tokens, 0).astype(F32)).astype(BF)
+        dq_all = jnp.concatenate([dq, cross(dq, 0)], 0)
+        e1 = (
+            e1
+            + dot(dq, w[:, :hw], 1, 1)
+            + dot(dk_all[:tokens], w[:, hw : 2 * hw], 1, 1)
+            + dot(dv_all[:tokens], w[:, 2 * hw : 3 * hw], 1, 1)
+        )
+        b_q.append(jnp.sum(dq.astype(F32), 0))
+        b_v.append(jnp.sum(dv_all[:tokens].astype(F32), 0))
+        qkv_part = weight_grad_all(one_both, jnp.concatenate([dq_all, dk_all, dv_all], 1), r % 2 == 1)
+        o_part = weight_grad(gm_both, mixed, r % 2 == 0)
+        a_parts.append(jnp.concatenate([qkv_part, o_part], 1))
+    d_cells = d_middle + norm_back(e1, unit_one, inv_one, gain_one)
+    grad_cells = give_back(d_cells.astype(BF)).astype(F32)
+    grad_attn = finish(a_parts)
+
+    split_mp = [jnp.stack(b_q).reshape(n_mp, n_dp, -1), jnp.stack(b_v).reshape(n_mp, n_dp, -1), jnp.stack(b_up).reshape(n_mp, n_dp, -1)]
+    sums = [
+        vec[4],
+        jnp.sum(e1 * unit_one, 0),
+        jnp.sum(e1, 0),
+        vec[5],
+        vec[6],
+        vec[7],
     ]
     split_dp = [jnp.roll(jnp.swapaxes(s.reshape(n_dp, n_mp, -1), 0, 1), -z, 0) for s in sums]
     packed = jnp.concatenate(split_mp + split_dp, 2)

time: 874 us -> 741 us (0.85)
  Pallas kernels: 0 us -> 200 us
  local copies, waits for them, and re-layouts: 157 us -> 66.2 us
  matrix products: 193 us -> 124 us
  other arithmetic: 132 us -> 66.8 us
  waiting for transfers between devices: 233 us -> 173 us
  starting transfers between devices: 150 us -> 97.2 us
    pallas_call x0 -> x1, Pallas kernels: none -> 200 us  [forward(): pl.pallas_call(forward_kernel, out_shape=[s(o, F32 if n in wide else BF)...]
    dot_general x64 -> x24, matrix products: 113 us -> 43.7 us  [dot(): lax.dot_general(a, b, (((ca,), (cb,)), ((), ())), preferred_element_type=...]
    ppermute x100 -> x53, starting transfers between devices: 82.7 us -> 35.7 us  [cross(): return lax.ppermute(x, 'dp', [(i, i ^ 1 << bit) for i in range(n)])]
    ppermute x27 -> x12, waiting for transfers between devices: 84.8 us -> 38.8 us  [shift(): return lax.ppermute(x, 'mp', [(i, (i + by) % n) for i in range(n)])]
    unnamed x509 -> x178, local copies, waits for them, and re-layouts: 52.4 us -> 8.56 us
    ppermute x4, starting transfers between devices: 13.2 us -> 53 us  [give_back(): lax.ppermute(lax.dynamic_index_in_dim(x, (t + z) % slots, 0, False), ('dp...]
    sub x4 -> x0, matrix products: 28.1 us -> none  [attend(): e = jnp.exp(s - jnp.max(s, -1, keepdims=True))]
    ppermute x4 -> x0, starting transfers between devices: 25.3 us -> none  [bring(): lax.ppermute(lax.dynamic_index_in_dim(x, (t + z) % slots, 0, False), ('dp...]
  transfers between devices with their start and end apart: 135 -> 69, of which waited for: 48 -> 35; matrix products, arithmetic and copies ran while one was open for 53% -> 23% of each run, Pallas kernels for 0% -> 0%
where the time goes in v2:
time: 741 us; the launch traced here: 731 us
  Pallas kernels  200 us (27%)
  waiting for transfers between devices  173 us (23%)
  matrix products  124 us (17%)
  starting transfers between devices  97.2 us (13%)
  other arithmetic  66.8 us (9%)
  local copies, waits for them, and re-layouts  66.2 us (9%)
    pallas_call x1, Pallas kernels, forward(): pl.pallas_call(forward_kernel, out_shape=[s(o, F32 if n in wide else BF)...  200 us
    ppermute x53, waiting for transfers between devices, cross(): return lax.ppermute(x, 'dp', [(i, i ^ 1 << bit) for i in range(n)])  82.5 us
    ppermute x4, starting transfers between devices, give_back(): lax.ppermute(lax.dynamic_index_in_dim(x, (t + z) % slots, 0, False), ('dp...  53 us
    ppermute x4, waiting for transfers between devices, give_back(): lax.ppermute(lax.dynamic_index_in_dim(x, (t + z) % slots, 0, False), ('dp...  51.8 us
    dot_general x24, matrix products, dot(): lax.dot_general(a, b, (((ca,), (cb,)), ((), ())), preferred_element_type=...  43.7 us
    ppermute x12, waiting for transfers between devices, shift(): return lax.ppermute(x, 'mp', [(i, (i + by) % n) for i in range(n)])  38.8 us
    ppermute x53, starting transfers between devices, cross(): return lax.ppermute(x, 'dp', [(i, i ^ 1 << bit) for i in range(n)])  35.7 us
    dot_general x4, matrix products, attend_back(): dp = jnp.einsum('qhd,khd->hqk', dh, vh, preferred_element_type=F32)  33.9 us
  transfers between devices with their start and end apart: 69, of which 35 were waited for; matrix products, arithmetic and copies ran while one was open for 23% of the time, Pallas kernels for 0%

profile of v2, /device:TPU:9, one launch (start us, length us, event | category | flops | bytes accessed | tf_op | source)
XLA Modules:
  0.0 730.7 jit_solution(8320748932283308235)
XLA Ops:
  3.3 200.2 %shard_map.305 = (bf16[512,1024]{1,0:T(8,128)(2,1)}, bf16[512,1024]{1,0:T(8,128)(2,1)}, bf16[4,512,256]{2,1,0:T(8,128)(2,1)}, bf16[4,1024,256]{2,1,0:T(8,128)(2,...) custom-call(bf16[2,256,1024]{2,1,0:T(8,128)(2,1)} %cells.1, ...), custom_call_target="tpu_custom_call" | custom-call | tf_op jit(solution)/shard_map/pallas_call | solution.py:960
  217.3 2.2 fusion.186
  220.6 5.6 fusion.197
  226.3 4.5 fusion.198
  230.8 4.6 fusion.199
  235.5 19.1 %fusion.6 = (f32[4,512]{1,0:T(4,128)S(1)}, f32[4,512]{1,0:T(4,128)S(1)}, f32[4,512]{1,0:T(4,128)S(1)}, f32[4,512]{1,0:T(4,128)S(1)}, f32[4,512,1024]{1,2,0:T(8,128)}) fusion(f32[4,512]{1,0:T(4,128)S(1)} %get-tuple-element.249, bf16[16,1024,512]{2,1,0:T(8,128)(2,1)} %get-tuple-element.38, f32[4,512,1024]{1,2,0:T(8,128)} %fusion.199, ...), kind=kOutput, calls=%fused_computation.19 | convolution fusion | flops 318758912 | bytes 51183616 | tf_op jit(solution)/shard_map/qhd,khd->hqk/dot_general | solution.py:121
  254.6 23.2 %fusion.7 = (bf16[4,512,1024]{1,2,0:T(8,128)(2,1)S(1)}, bf16[4,512,1024]{1,2,0:T(8,128)(2,1)}, bf16[4,512,1024]{1,2,0:T(8,128)(2,1)}, bf16[4,512,1024]{1,2,0:T(8,128)(2,1)}) fusion(f32[4,512,1024]{1,2,0:T(8,128)} %get-tuple-element.232, f32[4,512]{1,0:T(4,128)S(1)} %get-tuple-element.100, f32[4,512]{1,0:T(4,128)S(1)} %get-tuple-element.249, ...), kind=kLoop, calls=%fused_computation.20 | loop fusion | flops 58720256 | bytes 67174400 | tf_op jit(solution)/shard_map/convert_element_type | solution.py:123
  279.8 2.2 fusion.68
  282.2 3.7 convert_reduce_fusion.8
  286.7 3.7 convert_reduce_fusion.7
  290.6 3.7 convert_reduce_fusion.6
  295.1 3.1 convert_reduce_fusion.5
  298.2 4.4 fusion.75
  302.6 4.4 fusion.74
  307.0 4.6 fusion.73
  312.4 2.4 copy_bitcast_fusion.1
  316.2 2.6 gather_fusion.2
  320.3 2.6 gather_fusion.1
  322.9 3.0 fusion.181
  327.9 5.0 slice_bitcast_fusion.3
  333.0 3.0 fusion.101
  336.0 2.7 fusion.95
  338.9 4.5 fusion.69
  343.3 3.0 fusion.89
  346.4 4.4 fusion.70
  350.8 3.0 fusion.83
  355.7 4.5 fusion.71
  361.8 2.3 select_bitcast_fusion.2
  366.2 2.3 select_bitcast_fusion.3
  372.6 2.0 copy.149
  374.7 2.4 fusion.185
  385.5 2.3 dynamic-slice_bitcast_fusion.3
  389.7 3.7 fusion.72
  411.0 4.6 fusion.22
  421.5 3.6 fusion.65
  427.8 3.6 fusion.62
  433.5 2.7 fusion.59
  440.6 2.4 fusion.21
  444.1 29.1 %collective-permute-start = (bf16[256,1024]{1,0:T(8,128)(2,1)S(1)}, bf16[256,1024]{1,0:T(8,128)(2,1)S(1)}, u32[]{:S(2)}, u32[]{:S(2)}) collective-permute-start(bf16[256,1024]{1,0:T(8,128)(2,1)S(1)} %copy-done.68), channel_id=1, source_target_pairs={{0,0},{1,1},{4,2},{5,3},{2,4},{3,5},{6,6},{7,7},{8,8},{9,9},{12,10... | collective-permute-start | bytes 1572872 | tf_op jit(solution)/shard_map/ppermute | solution.py:1030
  475.2 2.1 fusion.56
  477.4 8.7 %collective-permute-done = bf16[256,1024]{1,0:T(8,128)(2,1)S(1)} collective-permute-done((bf16[256,1024]{1,0:T(8,128)(2,1)S(1)}, bf16[256,1024]{1,0:T(8,128)(2,1)S(1)}, u32[]{:S(2)}, u32[]{:S(2)}) %collective-permute-start) | collective-permute-done | bytes 524320 | tf_op jit(solution)/shard_map/ppermute | solution.py:1030
  486.3 5.9 collective-permute-done.1
  496.6 3.2 collective-permute-start.47
  508.9 2.9 collective-permute-done.47
  512.9 10.1 %collective-permute-done.49 = bf16[2,128,1024]{2,1,0:T(8,128)(2,1)S(1)} collective-permute-done((bf16[2,128,1024]{2,1,0:T(8,128)(2,1)S(1)}, bf16[2,128,1024]{2,1,0:T(8,128)(2,1)S(1)}, u32[]{:S(2)}, u32[]{:S(2)}) %collective-permute-start.49) | collective-permute-done | bytes 524320 | tf_op jit(solution)/shard_map/ppermute | solution.py:23
  524.3 9.9 %collective-permute-done.52 = bf16[2,128,1024]{2,1,0:T(8,128)(2,1)S(1)} collective-permute-done((bf16[2,128,1024]{2,1,0:T(8,128)(2,1)S(1)}, bf16[2,128,1024]{2,1,0:T(8,128)(2,1)S(1)}, u32[]{:S(2)}, u32[]{:S(2)}) %collective-permute-start.52) | collective-permute-done | bytes 524320 | tf_op jit(solution)/shard_map/ppermute | solution.py:23
  534.3 11.2 %collective-permute-done.55 = bf16[2,128,1024]{2,1,0:T(8,128)(2,1)S(1)} collective-permute-done((bf16[2,128,1024]{2,1,0:T(8,128)(2,1)S(1)}, bf16[2,128,1024]{2,1,0:T(8,128)(2,1)S(1)}, u32[]{:S(2)}, u32[]{:S(2)}) %collective-permute-start.55) | collective-permute-done | bytes 524320 | tf_op jit(solution)/shard_map/ppermute | solution.py:23
  547.2 9.8 %collective-permute-done.42 = f32[2,4,384]{2,1,0:T(4,128)S(1)} collective-permute-done((f32[2,4,384]{2,1,0:T(4,128)S(1)}, f32[2,4,384]{2,1,0:T(4,128)S(1)}, u32[]{:S(2)}, u32[]{:S(2)}) %collective-permute-start.42) | collective-permute-done | bytes 12320 | tf_op jit(solution)/shard_map/ppermute | solution.py:23
  566.7 2.5 collective-permute-done.18
  569.2 6.1 collective-permute-done.24
  575.8 3.4 collective-permute-done.31
  580.0 3.2 collective-permute-done.38
  584.2 2.2 collective-permute-done.19
  590.4 3.0 collective-permute-done.32
  593.9 2.6 collective-permute-done.39
  602.5 2.1 collective-permute-done.53
  605.3 2.8 collective-permute-done.56
  609.0 23.9 %collective-permute-start.10 = (bf16[256,1024]{1,0:T(8,128)(2,1)S(1)}, bf16[256,1024]{1,0:T(8,128)(2,1)S(1)}, u32[]{:S(2)}, u32[]{:S(2)}) collective-permute-start(bf16[256,1024]{1,0:T(8,128)(2,1)S(1)} %get-tuple-element.168), channel_id=1, source_target_pairs={{0,0},{1,1},{4,2},{5,3},{2,4},{3,5},{6,6},{7,7},{8,8},{9,9},{12,10... | collective-permute-start | bytes 1572872 | tf_op jit(solution)/shard_map/ppermute | solution.py:1030
  635.5 17.3 %collective-permute-done.10 = bf16[256,1024]{1,0:T(8,128)(2,1)S(1)} collective-permute-done((bf16[256,1024]{1,0:T(8,128)(2,1)S(1)}, bf16[256,1024]{1,0:T(8,128)(2,1)S(1)}, u32[]{:S(2)}, u32[]{:S(2)}) %collective-permute-start.10) | collective-permute-done | bytes 524320 | tf_op jit(solution)/shard_map/ppermute | solution.py:1030
  652.8 19.9 %collective-permute-done.11 = bf16[256,1024]{1,0:T(8,128)(2,1)S(1)} collective-permute-done((bf16[256,1024]{1,0:T(8,128)(2,1)S(1)}, bf16[256,1024]{1,0:T(8,128)(2,1)S(1)}, u32[]{:S(2)}, u32[]{:S(2)}) %collective-permute-start.11) | collective-permute-done | bytes 524320 | tf_op jit(solution)/shard_map/ppermute | solution.py:1030
  676.1 14.0 %collective-permute-done.65 = bf16[128,1024]{1,0:T(8,128)(2,1)S(1)} collective-permute-done((bf16[128,1024]{1,0:T(8,128)(2,1)S(1)}, bf16[128,1024]{1,0:T(8,128)(2,1)S(1)}, u32[]{:S(2)}, u32[]{:S(2)}) %collective-permute-start.65) | collective-permute-done | bytes 262176 | tf_op jit(solution)/shard_map/ppermute | solution.py:28
  693.3 4.6 collective-permute-done.51
  703.7 2.4 collective-permute-start.33
  711.5 14.4 %collective-permute-done.33 = bf16[128,1024]{1,0:T(8,128)(2,1)} collective-permute-done((bf16[128,1024]{1,0:T(8,128)(2,1)S(1)}, bf16[128,1024]{1,0:T(8,128)(2,1)}, u32[]{:S(2)}, u32[]{:S(2)}) %collective-permute-start.33) | collective-permute-done | bytes 262176 | tf_op jit(solution)/shard_map/ppermute | solution.py:28
  (457 shorter events, 148.7 us)
Async XLA Ops:
  282.0 111.4 %collective-permute-start.2 = (bf16[1024,256]{0,1:T(8,128)(2,1)}, bf16[1024,256]{0,1:T(8,128)(2,1)}, u32[]{:S(2)}, u32[]{:S(2)}) collective-permute-start(bf16[1024,256]{0,1:T(8,128)(2,1)} %bitcast.20), channel_id=1, source_target_pairs={{0,4},{4,0},{8,12},{12,8},{16,20},{20,16},{24,28},{28,24},{1,5},{5... | collective-permute-start | bytes 1572872 | tf_op jit(solution)/shard_map/ppermute | solution.py:23
  286.0 134.0 %collective-permute-start.13 = (bf16[512,256]{0,1:T(8,128)(2,1)}, bf16[512,256]{0,1:T(8,128)(2,1)}, u32[]{:S(2)}, u32[]{:S(2)}) collective-permute-start(bf16[512,256]{0,1:T(8,128)(2,1)} %bitcast.16), channel_id=1, source_target_pairs={{0,4},{4,0},{8,12},{12,8},{16,20},{20,16},{24,28},{28,24},{1,5},{5... | collective-permute-start | bytes 786440 | tf_op jit(solution)/shard_map/ppermute | solution.py:23
  290.4 136.6 %collective-permute-start.20 = (bf16[512,256]{0,1:T(8,128)(2,1)}, bf16[512,256]{0,1:T(8,128)(2,1)}, u32[]{:S(2)}, u32[]{:S(2)}) collective-permute-start(bf16[512,256]{0,1:T(8,128)(2,1)} %bitcast.30), channel_id=1, source_target_pairs={{0,4},{4,0},{8,12},{12,8},{16,20},{20,16},{24,28},{28,24},{1,5},{5... | collective-permute-start | bytes 786440 | tf_op jit(solution)/shard_map/ppermute | solution.py:23
  294.3 139.1 %collective-permute-start.27 = (bf16[512,256]{0,1:T(8,128)(2,1)}, bf16[512,256]{0,1:T(8,128)(2,1)}, u32[]{:S(2)}, u32[]{:S(2)}) collective-permute-start(bf16[512,256]{0,1:T(8,128)(2,1)} %bitcast.44), channel_id=1, source_target_pairs={{0,4},{4,0},{8,12},{12,8},{16,20},{20,16},{24,28},{28,24},{1,5},{5... | collective-permute-start | bytes 786440 | tf_op jit(solution)/shard_map/ppermute | solution.py:23
  298.2 176.8 %collective-permute-start.34 = (bf16[512,256]{0,1:T(8,128)(2,1)S(1)}, bf16[512,256]{0,1:T(8,128)(2,1)}, u32[]{:S(2)}, u32[]{:S(2)}) collective-permute-start(bf16[512,256]{0,1:T(8,128)(2,1)S(1)} %bitcast.396), channel_id=1, source_target_pairs={{0,4},{4,0},{8,12},{12,8},{16,20},{20,16},{24,28},{28,24},{1,5},{5... | collective-permute-start | bytes 786440 | tf_op jit(solution)/shard_map/ppermute | solution.py:23
  393.4 4.2 collective-permute-start.4
  397.6 2.0 collective-permute-start.6
  401.5 2.1 collective-permute-start.3
  409.5 10.8 %collective-permute-start.12 = (bf16[512,512]{0,1:T(8,128)(2,1)}, bf16[512,512]{0,1:T(8,128)(2,1)}, u32[]{:S(2)}, u32[]{:S(2)}) collective-permute-start(bf16[512,512]{0,1:T(8,128)(2,1)} %bitcast.75), channel_id=1, source_target_pairs={{0,4},{4,0},{8,12},{12,8},{16,20},{20,16},{24,28},{28,24},{1,5},{5... | collective-permute-start | bytes 1572872 | tf_op jit(solution)/shard_map/ppermute | solution.py:23
  420.0 81.3 %collective-permute-start.58 = (bf16[2,128,1024]{2,1,0:T(8,128)(2,1)}, bf16[2,128,1024]{2,1,0:T(8,128)(2,1)}, u32[]{:S(2)}, u32[]{:S(2)}) collective-permute-start(bf16[2,128,1024]{2,1,0:T(8,128)(2,1)} %pad_maximum_fusion.7), channel_id=1, source_target_pairs={{0,16},{4,20},{8,24},{12,28},{16,0},{20,4},{24,8},{28,12},{1,17},{... | collective-permute-start | bytes 1572872 | tf_op jit(solution)/shard_map/ppermute | solution.py:23
  420.3 81.8 %collective-permute-start.60 = (bf16[2,128,1024]{2,1,0:T(8,128)(2,1)}, bf16[2,128,1024]{2,1,0:T(8,128)(2,1)}, u32[]{:S(2)}, u32[]{:S(2)}) collective-permute-start(bf16[2,128,1024]{2,1,0:T(8,128)(2,1)} %pad_maximum_fusion.8), channel_id=1, source_target_pairs={{0,16},{4,20},{8,24},{12,28},{16,0},{20,4},{24,8},{28,12},{1,17},{... | collective-permute-start | bytes 1572872 | tf_op jit(solution)/shard_map/ppermute | solution.py:23
  427.0 46.1 %collective-permute-start.16 = (bf16[512,512]{0,1:T(8,128)(2,1)}, bf16[512,512]{0,1:T(8,128)(2,1)}, u32[]{:S(2)}, u32[]{:S(2)}) collective-permute-start(bf16[512,512]{0,1:T(8,128)(2,1)} %bitcast.416), channel_id=1, source_target_pairs={{0,4},{4,0},{8,12},{12,8},{16,20},{20,16},{24,28},{28,24},{1,5},{5... | collective-permute-start | bytes 1572872 | tf_op jit(solution)/shard_map/ppermute | solution.py:23
  433.5 10.1 %collective-permute-start.17 = (bf16[512,256]{1,0:T(8,128)(2,1)}, bf16[512,256]{1,0:T(8,128)(2,1)}, u32[]{:S(2)}, u32[]{:S(2)}) collective-permute-start(bf16[512,256]{1,0:T(8,128)(2,1)} %get-tuple-element.162), channel_id=1, source_target_pairs={{0,4},{4,0},{8,12},{12,8},{16,20},{20,16},{24,28},{28,24},{1,5},{5... | collective-permute-start | bytes 786440 | tf_op jit(solution)/shard_map/ppermute | solution.py:23
  444.1 42.0 %collective-permute-start = (bf16[256,1024]{1,0:T(8,128)(2,1)S(1)}, bf16[256,1024]{1,0:T(8,128)(2,1)S(1)}, u32[]{:S(2)}, u32[]{:S(2)}) collective-permute-start(bf16[256,1024]{1,0:T(8,128)(2,1)S(1)} %copy-done.68), channel_id=1, source_target_pairs={{0,0},{1,1},{4,2},{5,3},{2,4},{3,5},{6,6},{7,7},{8,8},{9,9},{12,10... | collective-permute-start | bytes 1572872 | tf_op jit(solution)/shard_map/ppermute | solution.py:1030
  473.2 19.0 %collective-permute-start.1 = (bf16[256,1024]{1,0:T(8,128)(2,1)S(1)}, bf16[256,1024]{1,0:T(8,128)(2,1)S(1)}, u32[]{:S(2)}, u32[]{:S(2)}) collective-permute-start(bf16[256,1024]{1,0:T(8,128)(2,1)S(1)} %copy-done.67), channel_id=1, source_target_pairs={{1,0},{0,1},{5,2},{4,3},{3,4},{2,5},{7,6},{6,7},{9,8},{8,9},{13,10... | collective-permute-start | bytes 1572872 | tf_op jit(solution)/shard_map/ppermute | solution.py:1030
  474.9 27.9 %collective-permute-start.63 = (bf16[2,128,1024]{2,1,0:T(8,128)(2,1)S(1)}, bf16[2,128,1024]{2,1,0:T(8,128)(2,1)S(1)}, u32[]{:S(2)}, u32[]{:S(2)}) collective-permute-start(bf16[2,128,1024]{2,1,0:T(8,128)(2,1)S(1)} %copy-done.65), channel_id=1, source_target_pairs={{0,16},{4,20},{8,24},{12,28},{16,0},{20,4},{24,8},{28,12},{1,17},{... | collective-permute-start | bytes 1572872 | tf_op jit(solution)/shard_map/ppermute | solution.py:23
  486.1 17.5 %collective-permute-start.66 = (bf16[2,128,1024]{2,1,0:T(8,128)(2,1)S(1)}, bf16[2,128,1024]{2,1,0:T(8,128)(2,1)S(1)}, u32[]{:S(2)}, u32[]{:S(2)}) collective-permute-start(bf16[2,128,1024]{2,1,0:T(8,128)(2,1)S(1)} %copy-done.64), channel_id=1, source_target_pairs={{0,16},{4,20},{8,24},{12,28},{16,0},{20,4},{24,8},{28,12},{1,17},{... | collective-permute-start | bytes 1572872 | tf_op jit(solution)/shard_map/ppermute | solution.py:23
  493.8 2.8 collective-permute-start.30
  496.6 15.2 %collective-permute-start.47 = (bf16[2,128,1024]{2,1,0:T(8,128)(2,1)S(1)}, bf16[2,128,1024]{2,1,0:T(8,128)(2,1)S(1)}, u32[]{:S(2)}, u32[]{:S(2)}) collective-permute-start(bf16[2,128,1024]{2,1,0:T(8,128)(2,1)S(1)} %copy-done.62), channel_id=1, source_target_pairs={{0,8},{4,12},{8,0},{12,4},{16,24},{20,28},{24,16},{28,20},{1,9},{5... | collective-permute-start | bytes 1572872 | tf_op jit(solution)/shard_map/ppermute | solution.py:23
  501.3 21.7 %collective-permute-start.49 = (bf16[2,128,1024]{2,1,0:T(8,128)(2,1)S(1)}, bf16[2,128,1024]{2,1,0:T(8,128)(2,1)S(1)}, u32[]{:S(2)}, u32[]{:S(2)}) collective-permute-start(bf16[2,128,1024]{2,1,0:T(8,128)(2,1)S(1)} %copy-done.61), channel_id=1, source_target_pairs={{0,8},{4,12},{8,0},{12,4},{16,24},{20,28},{24,16},{28,20},{1,9},{5... | collective-permute-start | bytes 1572872 | tf_op jit(solution)/shard_map/ppermute | solution.py:23
  502.2 32.1 %collective-permute-start.52 = (bf16[2,128,1024]{2,1,0:T(8,128)(2,1)S(1)}, bf16[2,128,1024]{2,1,0:T(8,128)(2,1)S(1)}, u32[]{:S(2)}, u32[]{:S(2)}) collective-permute-start(bf16[2,128,1024]{2,1,0:T(8,128)(2,1)S(1)} %copy-done.60), channel_id=1, source_target_pairs={{0,8},{4,12},{8,0},{12,4},{16,24},{20,28},{24,16},{28,20},{1,9},{5... | collective-permute-start | bytes 1572872 | tf_op jit(solution)/shard_map/ppermute | solution.py:23
  502.8 42.6 %collective-permute-start.55 = (bf16[2,128,1024]{2,1,0:T(8,128)(2,1)S(1)}, bf16[2,128,1024]{2,1,0:T(8,128)(2,1)S(1)}, u32[]{:S(2)}, u32[]{:S(2)}) collective-permute-start(bf16[2,128,1024]{2,1,0:T(8,128)(2,1)S(1)} %copy-done.63), channel_id=1, source_target_pairs={{0,8},{4,12},{8,0},{12,4},{16,24},{20,28},{24,16},{28,20},{1,9},{5... | collective-permute-start | bytes 1572872 | tf_op jit(solution)/shard_map/ppermute | solution.py:23
  503.6 2.7 collective-permute-start.37
  506.4 90.6 %collective-permute-start.61 = (bf16[1,128,1024]{2,1,0:T(8,128)(2,1)S(1)}, bf16[1,128,1024]{2,1,0:T(8,128)(2,1)S(1)}, u32[]{:S(2)}, u32[]{:S(2)}) collective-permute-start(bf16[1,128,1024]{2,1,0:T(8,128)(2,1)S(1)} %get-tuple-element.127), channel_id=1, source_target_pairs={{0,8},{4,12},{8,0},{12,4},{16,24},{20,28},{24,16},{28,20},{1,9},{5... | collective-permute-start | bytes 786440 | tf_op jit(solution)/shard_map/ppermute | solution.py:23
  511.8 86.3 %collective-permute-start.64 = (bf16[1,128,1024]{2,1,0:T(8,128)(2,1)S(1)}, bf16[1,128,1024]{2,1,0:T(8,128)(2,1)S(1)}, u32[]{:S(2)}, u32[]{:S(2)}) collective-permute-start(bf16[1,128,1024]{2,1,0:T(8,128)(2,1)S(1)} %get-tuple-element.126), channel_id=1, source_target_pairs={{0,8},{4,12},{8,0},{12,4},{16,24},{20,28},{24,16},{28,20},{1,9},{5... | collective-permute-start | bytes 786440 | tf_op jit(solution)/shard_map/ppermute | solution.py:23
  523.0 22.9 %collective-permute-start.41 = (f32[4,4,384]{2,0,1:T(4,128)S(1)}, f32[4,4,384]{2,0,1:T(4,128)S(1)}, u32[]{:S(2)}, u32[]{:S(2)}) collective-permute-start(f32[4,4,384]{2,0,1:T(4,128)S(1)} %slice.869), channel_id=1, source_target_pairs={{0,4},{4,0},{8,12},{12,8},{16,20},{20,16},{24,28},{28,24},{1,5},{5... | collective-permute-start | bytes 73736 | tf_op jit(solution)/shard_map/ppermute | solution.py:23
  546.0 11.0 %collective-permute-start.42 = (f32[2,4,384]{2,1,0:T(4,128)S(1)}, f32[2,4,384]{2,1,0:T(4,128)S(1)}, u32[]{:S(2)}, u32[]{:S(2)}) collective-permute-start(f32[2,4,384]{2,1,0:T(4,128)S(1)} %pad_maximum_fusion.24), channel_id=1, source_target_pairs={{0,8},{4,12},{8,0},{12,4},{16,24},{20,28},{24,16},{28,20},{1,9},{5... | collective-permute-start | bytes 36872 | tf_op jit(solution)/shard_map/ppermute | solution.py:23
  557.0 2.5 collective-permute-start.43
  559.5 2.5 collective-permute-start.44
  560.5 3.3 collective-permute-start.45
  560.5 4.5 collective-permute-start.46
  562.1 36.6 %collective-permute-start.67 = (bf16[1,128,1024]{2,1,0:T(8,128)(2,1)S(1)}, bf16[1,128,1024]{2,1,0:T(8,128)(2,1)S(1)}, u32[]{:S(2)}, u32[]{:S(2)}) collective-permute-start(bf16[1,128,1024]{2,1,0:T(8,128)(2,1)S(1)} %get-tuple-element.125), channel_id=1, source_target_pairs={{0,8},{4,12},{8,0},{12,4},{16,24},{20,28},{24,16},{28,20},{1,9},{5... | collective-permute-start | bytes 786440 | tf_op jit(solution)/shard_map/ppermute | solution.py:23
  563.9 108.9 %collective-permute-start.59 = (bf16[1,128,1024]{2,1,0:T(8,128)(2,1)S(1)}, bf16[1,128,1024]{2,1,0:T(8,128)(2,1)S(1)}, u32[]{:S(2)}, u32[]{:S(2)}) collective-permute-start(bf16[1,128,1024]{2,1,0:T(8,128)(2,1)S(1)} %get-tuple-element.124), channel_id=1, source_target_pairs={{0,8},{4,12},{8,0},{12,4},{16,24},{20,28},{24,16},{28,20},{1,9},{5... | collective-permute-start | bytes 786440 | tf_op jit(solution)/shard_map/ppermute | solution.py:23
  565.0 4.1 collective-permute-start.18
  569.1 6.2 collective-permute-start.24
  575.3 3.8 collective-permute-start.31
  579.1 4.1 collective-permute-start.38
  583.2 3.1 collective-permute-start.19
  586.4 3.1 collective-permute-start.25
  589.5 3.9 collective-permute-start.32
  593.4 3.1 collective-permute-start.39
  596.5 5.5 collective-permute-start.50
  597.0 7.6 %collective-permute-start.53 = (bf16[1,128,1024]{2,1,0:T(8,128)(2,1)S(1)}, bf16[1,128,1024]{2,1,0:T(8,128)(2,1)S(1)}, u32[]{:S(2)}, u32[]{:S(2)}) collective-permute-start(bf16[1,128,1024]{2,1,0:T(8,128)(2,1)S(1)} %get-tuple-element.141), channel_id=1, source_target_pairs={{0,16},{4,20},{8,24},{12,28},{16,0},{20,4},{24,8},{28,12},{1,17},{... | collective-permute-start | bytes 786440 | tf_op jit(solution)/shard_map/ppermute | solution.py:23
  598.1 10.0 %collective-permute-start.56 = (bf16[1,128,1024]{2,1,0:T(8,128)(2,1)S(1)}, bf16[1,128,1024]{2,1,0:T(8,128)(2,1)S(1)}, u32[]{:S(2)}, u32[]{:S(2)}) collective-permute-start(bf16[1,128,1024]{2,1,0:T(8,128)(2,1)S(1)} %get-tuple-element.140), channel_id=1, source_target_pairs={{0,16},{4,20},{8,24},{12,28},{16,0},{20,4},{24,8},{28,12},{1,17},{... | collective-permute-start | bytes 786440 | tf_op jit(solution)/shard_map/ppermute | solution.py:23
  598.6 10.3 %collective-permute-start.14 = (bf16[2,128,768]{2,1,0:T(8,128)(2,1)S(1)}, bf16[2,128,768]{2,1,0:T(8,128)(2,1)S(1)}, u32[]{:S(2)}, u32[]{:S(2)}) collective-permute-start(bf16[2,128,768]{2,1,0:T(8,128)(2,1)S(1)} %pad_maximum_fusion.11), channel_id=1, source_target_pairs={{0,8},{4,12},{8,0},{12,4},{16,24},{20,28},{24,16},{28,20},{1,9},{5... | collective-permute-start | bytes 1179656 | tf_op jit(solution)/shard_map/ppermute | solution.py:23
  602.0 31.6 %collective-permute-start.21 = (bf16[2,128,768]{2,1,0:T(8,128)(2,1)S(1)}, bf16[2,128,768]{2,1,0:T(8,128)(2,1)S(1)}, u32[]{:S(2)}, u32[]{:S(2)}) collective-permute-start(bf16[2,128,768]{2,1,0:T(8,128)(2,1)S(1)} %pad_maximum_fusion.12), channel_id=1, source_target_pairs={{0,16},{4,20},{8,24},{12,28},{16,0},{20,4},{24,8},{28,12},{1,17},{... | collective-permute-start | bytes 1179656 | tf_op jit(solution)/shard_map/ppermute | solution.py:23
  604.6 29.1 %collective-permute-start.28 = (bf16[2,128,768]{2,1,0:T(8,128)(2,1)S(1)}, bf16[2,128,768]{2,1,0:T(8,128)(2,1)S(1)}, u32[]{:S(2)}, u32[]{:S(2)}) collective-permute-start(bf16[2,128,768]{2,1,0:T(8,128)(2,1)S(1)} %pad_maximum_fusion.13), channel_id=1, source_target_pairs={{0,8},{4,12},{8,0},{12,4},{16,24},{20,28},{24,16},{28,20},{1,9},{5... | collective-permute-start | bytes 1179656 | tf_op jit(solution)/shard_map/ppermute | solution.py:23
  608.1 27.3 %collective-permute-start.35 = (bf16[2,128,768]{2,1,0:T(8,128)(2,1)S(1)}, bf16[2,128,768]{2,1,0:T(8,128)(2,1)S(1)}, u32[]{:S(2)}, u32[]{:S(2)}) collective-permute-start(bf16[2,128,768]{2,1,0:T(8,128)(2,1)S(1)} %pad_maximum_fusion.14), channel_id=1, source_target_pairs={{0,16},{4,20},{8,24},{12,28},{16,0},{20,4},{24,8},{28,12},{1,17},{... | collective-permute-start | bytes 1179656 | tf_op jit(solution)/shard_map/ppermute | solution.py:23
  609.0 43.8 %collective-permute-start.10 = (bf16[256,1024]{1,0:T(8,128)(2,1)S(1)}, bf16[256,1024]{1,0:T(8,128)(2,1)S(1)}, u32[]{:S(2)}, u32[]{:S(2)}) collective-permute-start(bf16[256,1024]{1,0:T(8,128)(2,1)S(1)} %get-tuple-element.168), channel_id=1, source_target_pairs={{0,0},{1,1},{4,2},{5,3},{2,4},{3,5},{6,6},{7,7},{8,8},{9,9},{12,10... | collective-permute-start | bytes 1572872 | tf_op jit(solution)/shard_map/ppermute | solution.py:1030
  633.6 39.1 %collective-permute-start.11 = (bf16[256,1024]{1,0:T(8,128)(2,1)S(1)}, bf16[256,1024]{1,0:T(8,128)(2,1)S(1)}, u32[]{:S(2)}, u32[]{:S(2)}) collective-permute-start(bf16[256,1024]{1,0:T(8,128)(2,1)S(1)} %get-tuple-element.169), channel_id=1, source_target_pairs={{1,0},{0,1},{5,2},{4,3},{3,4},{2,5},{7,6},{6,7},{9,8},{8,9},{13,10... | collective-permute-start | bytes 1572872 | tf_op jit(solution)/shard_map/ppermute | solution.py:1030
  633.7 59.0 %collective-permute-start.48 = (bf16[1,128,1024]{2,1,0:T(8,128)(2,1)S(1)}, bf16[1,128,1024]{2,1,0:T(8,128)(2,1)S(1)}, u32[]{:S(2)}, u32[]{:S(2)}) collective-permute-start(bf16[1,128,1024]{2,1,0:T(8,128)(2,1)S(1)} %get-tuple-element.139), channel_id=1, source_target_pairs={{0,16},{4,20},{8,24},{12,28},{16,0},{20,4},{24,8},{28,12},{1,17},{... | collective-permute-start | bytes 786440 | tf_op jit(solution)/shard_map/ppermute | solution.py:23
  635.4 40.8 %collective-permute-start.62 = (bf16[128,1024]{1,0:T(8,128)(2,1)S(1)}, bf16[128,1024]{1,0:T(8,128)(2,1)S(1)}, u32[]{:S(2)}, u32[]{:S(2)}) collective-permute-start(bf16[128,1024]{1,0:T(8,128)(2,1)S(1)} %get-tuple-element.136), channel_id=1, source_target_pairs={{0,1},{1,2},{2,3},{3,0},{4,5},{5,6},{6,7},{7,4},{8,9},{9,10},{10,1... | collective-permute-start | bytes 786440 | tf_op jit(solution)/shard_map/ppermute | solution.py:28
  652.8 37.4 %collective-permute-start.65 = (bf16[128,1024]{1,0:T(8,128)(2,1)S(1)}, bf16[128,1024]{1,0:T(8,128)(2,1)S(1)}, u32[]{:S(2)}, u32[]{:S(2)}) collective-permute-start(bf16[128,1024]{1,0:T(8,128)(2,1)S(1)} %get-tuple-element.138), channel_id=1, source_target_pairs={{0,2},{1,3},{2,0},{3,1},{4,6},{5,7},{6,4},{7,5},{8,10},{9,11},{10,... | collective-permute-start | bytes 786440 | tf_op jit(solution)/shard_map/ppermute | solution.py:28
  672.7 17.5 %collective-permute-start.68 = (bf16[128,1024]{1,0:T(8,128)(2,1)S(1)}, bf16[128,1024]{1,0:T(8,128)(2,1)S(1)}, u32[]{:S(2)}, u32[]{:S(2)}) collective-permute-start(bf16[128,1024]{1,0:T(8,128)(2,1)S(1)} %get-tuple-element.137), channel_id=1, source_target_pairs={{0,3},{1,0},{2,1},{3,2},{4,7},{5,4},{6,5},{7,6},{8,11},{9,8},{10,9... | collective-permute-start | bytes 786440 | tf_op jit(solution)/shard_map/ppermute | solution.py:28
  672.8 25.2 %collective-permute-start.51 = (bf16[128,1024]{1,0:T(8,128)(2,1)S(1)}, bf16[128,1024]{1,0:T(8,128)(2,1)S(1)}, u32[]{:S(2)}, u32[]{:S(2)}) collective-permute-start(bf16[128,1024]{1,0:T(8,128)(2,1)S(1)} %get-tuple-element.151), channel_id=1, source_target_pairs={{0,1},{1,2},{2,3},{3,0},{4,5},{5,6},{6,7},{7,4},{8,9},{9,10},{10,1... | collective-permute-start | bytes 786440 | tf_op jit(solution)/shard_map/ppermute | solution.py:28
  676.1 24.6 %collective-permute-start.54 = (bf16[128,1024]{1,0:T(8,128)(2,1)S(1)}, bf16[128,1024]{1,0:T(8,128)(2,1)S(1)}, u32[]{:S(2)}, u32[]{:S(2)}) collective-permute-start(bf16[128,1024]{1,0:T(8,128)(2,1)S(1)} %get-tuple-element.153), channel_id=1, source_target_pairs={{0,2},{1,3},{2,0},{3,1},{4,6},{5,7},{6,4},{7,5},{8,10},{9,11},{10,... | collective-permute-start | bytes 786440 | tf_op jit(solution)/shard_map/ppermute | solution.py:28
  690.2 11.8 %collective-permute-start.57 = (bf16[128,1024]{1,0:T(8,128)(2,1)S(1)}, bf16[128,1024]{1,0:T(8,128)(2,1)S(1)}, u32[]{:S(2)}, u32[]{:S(2)}) collective-permute-start(bf16[128,1024]{1,0:T(8,128)(2,1)S(1)} %get-tuple-element.152), channel_id=1, source_target_pairs={{0,3},{1,0},{2,1},{3,2},{4,7},{5,4},{6,5},{7,6},{8,11},{9,8},{10,9... | collective-permute-start | bytes 786440 | tf_op jit(solution)/shard_map/ppermute | solution.py:28
  690.2 20.1 %collective-permute-start.15 = (bf16[1,128,768]{2,1,0:T(8,128)(2,1)}, bf16[1,128,768]{2,1,0:T(8,128)(2,1)}, u32[]{:S(2)}, u32[]{:S(2)}) collective-permute-start(bf16[1,128,768]{2,1,0:T(8,128)(2,1)} %fusion.134), channel_id=1, source_target_pairs={{0,16},{4,20},{8,24},{12,28},{16,0},{20,4},{24,8},{28,12},{1,17},{... | collective-permute-start | bytes 589832 | tf_op jit(solution)/shard_map/ppermute | solution.py:23
  692.7 10.3 %collective-permute-start.22 = (bf16[1,128,768]{2,1,0:T(8,128)(2,1)S(1)}, bf16[1,128,768]{2,1,0:T(8,128)(2,1)S(1)}, u32[]{:S(2)}, u32[]{:S(2)}) collective-permute-start(bf16[1,128,768]{2,1,0:T(8,128)(2,1)S(1)} %fusion.131), channel_id=1, source_target_pairs={{0,8},{4,12},{8,0},{12,4},{16,24},{20,28},{24,16},{28,20},{1,9},{5... | collective-permute-start | bytes 589832 | tf_op jit(solution)/shard_map/ppermute | solution.py:23
  697.9 5.6 collective-permute-start.29
  700.8 5.4 collective-permute-start.36
  703.1 8.4 %collective-permute-start.26 = (bf16[128,1024]{1,0:T(8,128)(2,1)S(1)}, bf16[128,1024]{1,0:T(8,128)(2,1)}, u32[]{:S(2)}, u32[]{:S(2)}) collective-permute-start(bf16[128,1024]{1,0:T(8,128)(2,1)S(1)} %pad_maximum_fusion.15), channel_id=1, source_target_pairs={{0,1},{1,2},{2,3},{3,0},{4,5},{5,6},{6,7},{7,4},{8,9},{9,10},{10,1... | collective-permute-start | bytes 786440 | tf_op jit(solution)/shard_map/ppermute | solution.py:28
  703.7 22.2 %collective-permute-start.33 = (bf16[128,1024]{1,0:T(8,128)(2,1)S(1)}, bf16[128,1024]{1,0:T(8,128)(2,1)}, u32[]{:S(2)}, u32[]{:S(2)}) collective-permute-start(bf16[128,1024]{1,0:T(8,128)(2,1)S(1)} %pad_maximum_fusion.16), channel_id=1, source_target_pairs={{0,2},{1,3},{2,0},{3,1},{4,6},{5,7},{6,4},{7,5},{8,10},{9,11},{10,... | collective-permute-start | bytes 786440 | tf_op jit(solution)/shard_map/ppermute | solution.py:28
  706.3 21.4 %collective-permute-start.40 = (bf16[128,1024]{1,0:T(8,128)(2,1)S(1)}, bf16[128,1024]{1,0:T(8,128)(2,1)S(1)}, u32[]{:S(2)}, u32[]{:S(2)}) collective-permute-start(bf16[128,1024]{1,0:T(8,128)(2,1)S(1)} %pad_maximum_fusion.17), channel_id=1, source_target_pairs={{0,3},{1,0},{2,1},{3,2},{4,7},{5,4},{6,5},{7,6},{8,11},{9,8},{10,9... | collective-permute-start | bytes 786440 | tf_op jit(solution)/shard_map/ppermute | solution.py:28
  (92 other events, 830.7 us)
